TPU v7x, 32 devices: a whole 2x2x4 slice. The times are simulated.
32 devices in a mesh: groups: 2 (over x), tiles: 16 (over z, y, core).
Axes of the slice: x: 2, y: 2, z: 4, core: 2. Of those that a mesh axis runs over, the one named last changes fastest.
Arguments:
- embeddings: bfloat16 [4096, 4096], P(('groups', 'tiles')), parts along dimension 0, may hold values from -6 to 6
- cluster_tiles: int32 [12], P('groups'), parts along dimension 0, may hold values from 1 to 8, 16 in all
- last_tile_pad: int32 [12], P('groups'), parts along dimension 0, may hold values from 0 to 126
Outputs:
- neighbour_sums: bfloat16 [4096, 4096], P(('groups', 'tiles')), parts along dimension 0
There are 2 independent parts, one for each index of `groups`. A program takes and returns all parts, laid end to end along the dimension named above; each array names one. Nothing has to cross between parts.
Inputs may be any that keep to these rules, and one draw needn't show every extreme that they name: `cluster_tiles`: whole numbers summing to 16; the largest is exactly 8. `last_tile_pad`: every cluster has two or more documents.
All inputs are finite; a program needn't handle non-finite values.
Results may differ from a plain program's by a relative error of at most 0.0085.
Values may be sent and summed in bfloat16 or wider, within the bound.
No kernel may reach another device: no remote copies, remote signals or barrier semaphores. Data moves between devices by JAX's collectives and lax.ppermute only.
A program may use at most 128 MiB of HBM per device.

v0:
```python
import jax
import jax.numpy as jnp
from jax import lax
from jax.sharding import PartitionSpec as P

MOST = 8


similarity_scale = 64.0


def shifted(value, axis, steps):
    count = lax.axis_size(axis)
    first, last = (max(0, -steps), min(count, count - steps))
    return lax.ppermute(value, axis, [(source, source + steps) for source in range(first, last)])


def tile_layout(cluster_tiles, last_tile_pad, tile_index, row_count):
    starts = jnp.cumsum(cluster_tiles) - cluster_tiles
    inside = (starts <= tile_index) & (tile_index < starts + cluster_tiles)
    cluster_ids = jnp.arange(cluster_tiles.shape[0], dtype=jnp.int32)
    present = jnp.any(inside)
    cluster_id = jnp.sum(jnp.where(inside, cluster_ids, 0))
    cluster_id = jnp.where(present, cluster_id, -1)
    cluster_size = cluster_tiles * row_count - last_tile_pad
    live_rows = jnp.sum(jnp.where(inside, cluster_size - (tile_index - starts) * row_count, 0))
    live_rows = jnp.clip(live_rows, 0, row_count)
    return (cluster_id, live_rows)


def inverse_norms(block):
    squares = jnp.einsum("ij,ij->i", block, block, preferred_element_type=jnp.float32)
    return lax.rsqrt(squares + 1e-06)


def pair_weights(own_block, inv_own, own_live, other_block, inv_other, other_live, diagonal):
    row_count = own_block.shape[0]
    gram = lax.dot_general(
        own_block, other_block, (((1,), (1,)), ((), ())), preferred_element_type=jnp.float32
    )
    row_ids = jnp.arange(row_count, dtype=jnp.int32)
    keep_mask = (row_ids[:, None] < own_live) & (row_ids[None, :] < other_live)
    if diagonal:
        keep_mask = keep_mask & (row_ids[:, None] != row_ids[None, :])
    scores = similarity_scale * inv_own[:, None] * inv_other[None, :] * gram
    return jnp.where(keep_mask, jnp.exp(scores), 0.0).astype(jnp.bfloat16)


def body(embeddings, cluster_tiles, last_tile_pad):
    row_count = embeddings.shape[0]
    width = embeddings.shape[1]
    own_index = lax.axis_index("tiles")
    inv_own = inverse_norms(embeddings)
    own_cluster, own_live = tile_layout(cluster_tiles, last_tile_pad, own_index, row_count)
    local_weights = pair_weights(embeddings, inv_own, own_live, embeddings, inv_own, own_live, True)
    numer_total = (
        jnp.dot(local_weights, embeddings, preferred_element_type=jnp.float32)
        .astype(jnp.bfloat16)
        .astype(jnp.float32)
    )
    denom_total = jnp.sum(local_weights.astype(jnp.float32), axis=1)
    for distance in range(-(MOST - 1), MOST):
        if distance == 0:
            continue
        other_block = shifted(embeddings, "tiles", -distance)
        other_cluster, other_live = tile_layout(
            cluster_tiles, last_tile_pad, own_index + distance, row_count
        )
        same_cluster = (own_cluster == other_cluster) & (other_cluster >= 0)

        def compute_pair(other_block=other_block, other_live=other_live):
            weights = pair_weights(
                embeddings,
                inv_own,
                own_live,
                other_block,
                inverse_norms(other_block),
                other_live,
                False,
            )
            block_sum = jnp.dot(weights, other_block, preferred_element_type=jnp.float32).astype(
                jnp.bfloat16
            )
            return (block_sum, jnp.sum(weights.astype(jnp.float32), axis=1))

        def skip_pair():
            return (
                jnp.zeros((row_count, width), jnp.bfloat16),
                jnp.zeros((row_count,), jnp.float32),
            )

        block_sum, weight_sum = lax.cond(same_cluster, compute_pair, skip_pair)
        numer_total = numer_total + block_sum.astype(jnp.float32)
        denom_total = denom_total + weight_sum
    live_mask = jnp.arange(row_count, dtype=jnp.int32) < own_live
    safe_denom = jnp.where(live_mask, denom_total, 1.0)
    result = jnp.where(live_mask[:, None], numer_total / safe_denom[:, None], 0.0)
    return result.astype(jnp.bfloat16)


def solution(mesh):
    placed = (P(("groups", "tiles"), None), P("groups"), P("groups"))
    return jax.shard_map(
        body, mesh=mesh, in_specs=placed, out_specs=P(("groups", "tiles"), None), check_vma=False
    )
```

profile of v0, /device:TPU:17, one launch (start us, length us, event | category | flops | bytes accessed | tf_op | source)
XLA Modules:
  0.0 316.5 jit_solution(13233693418357942677)
XLA Ops:
  0.0 4.3 %collective-permute-start.1 = (bf16[128,4096]{1,0:T(8,128)(2,1)}, bf16[128,4096]{1,0:T(8,128)(2,1)S(1)}, u32[]{:S(2)}, u32[]{:S(2)}) collective-permute-start(bf16[128,4096]{1,0:T(8,128)(2,1)} %param.31), channel_id=1, source_target_pairs={{0,6},{1,7},{2,8},{3,9},{4,10},{5,11},{6,12},{7,13},{8,14},{9,15},... | collective-permute-start | bytes 3145736 | tf_op jit(solution)/shard_map/ppermute | solution.py:15
  4.3 1.9 collective-permute-start.2
  6.2 1.9 collective-permute-start.3
  8.2 1.9 collective-permute-start.4
  10.1 1.9 collective-permute-start.5
  12.0 16.1 %collective-permute-done.1 = bf16[128,4096]{1,0:T(8,128)(2,1)S(1)} collective-permute-done((bf16[128,4096]{1,0:T(8,128)(2,1)}, bf16[128,4096]{1,0:T(8,128)(2,1)S(1)}, u32[]{:S(2)}, u32[]{:S(2)}) %collective-permute-start.1) | collective-permute-done | bytes 1048608 | tf_op jit(solution)/shard_map/ppermute | solution.py:15
  28.1 4.9 %collective-permute-start.6 = (bf16[128,4096]{1,0:T(8,128)(2,1)}, bf16[128,4096]{1,0:T(8,128)(2,1)}, u32[]{:S(2)}, u32[]{:S(2)}) collective-permute-start(bf16[128,4096]{1,0:T(8,128)(2,1)} %param.31), channel_id=1, source_target_pairs={{0,1},{1,2},{2,3},{3,4},{4,5},{5,6},{6,7},{7,8},{8,9},{9,10},{10,1... | collective-permute-start | bytes 3145736 | tf_op jit(solution)/shard_map/ppermute | solution.py:15
  33.0 18.7 %collective-permute-done.2 = bf16[128,4096]{1,0:T(8,128)(2,1)S(1)} collective-permute-done((bf16[128,4096]{1,0:T(8,128)(2,1)}, bf16[128,4096]{1,0:T(8,128)(2,1)S(1)}, u32[]{:S(2)}, u32[]{:S(2)}) %collective-permute-start.2) | collective-permute-done | bytes 1048608 | tf_op jit(solution)/shard_map/ppermute | solution.py:15
  51.7 1.9 collective-permute-start.7
  53.7 18.5 %collective-permute-done.3 = bf16[128,4096]{1,0:T(8,128)(2,1)S(1)} collective-permute-done((bf16[128,4096]{1,0:T(8,128)(2,1)}, bf16[128,4096]{1,0:T(8,128)(2,1)S(1)}, u32[]{:S(2)}, u32[]{:S(2)}) %collective-permute-start.3) | collective-permute-done | bytes 1048608 | tf_op jit(solution)/shard_map/ppermute | solution.py:15
  72.2 36.9 %collective-permute-start.8 = (bf16[128,4096]{1,0:T(8,128)(2,1)}, bf16[128,4096]{1,0:T(8,128)(2,1)S(1)}, u32[]{:S(2)}, u32[]{:S(2)}) collective-permute-start(bf16[128,4096]{1,0:T(8,128)(2,1)} %param.31), channel_id=1, source_target_pairs={{2,0},{3,1},{4,2},{5,3},{6,4},{7,5},{8,6},{9,7},{10,8},{11,9},{12,... | collective-permute-start | bytes 3145736 | tf_op jit(solution)/shard_map/ppermute | solution.py:15
  109.1 21.3 %collective-permute-done.4 = bf16[128,4096]{1,0:T(8,128)(2,1)} collective-permute-done((bf16[128,4096]{1,0:T(8,128)(2,1)}, bf16[128,4096]{1,0:T(8,128)(2,1)}, u32[]{:S(2)}, u32[]{:S(2)}) %collective-permute-start.4) | collective-permute-done | bytes 1048608 | tf_op jit(solution)/shard_map/ppermute | solution.py:15
  130.4 1.9 collective-permute-start.9
  165.5 1.9 collective-permute-start.10
  167.4 1.9 collective-permute-start.11
  169.3 1.9 collective-permute-start.12
  171.3 5.6 %collective-permute-done.8 = bf16[128,4096]{1,0:T(8,128)(2,1)S(1)} collective-permute-done((bf16[128,4096]{1,0:T(8,128)(2,1)}, bf16[128,4096]{1,0:T(8,128)(2,1)S(1)}, u32[]{:S(2)}, u32[]{:S(2)}) %collective-permute-start.8) | collective-permute-done | bytes 1048608 | tf_op jit(solution)/shard_map/ppermute | solution.py:15
  178.2 7.1 %collective-permute-start.13 = (bf16[128,4096]{1,0:T(8,128)(2,1)}, bf16[128,4096]{1,0:T(8,128)(2,1)S(1)}, u32[]{:S(2)}, u32[]{:S(2)}) collective-permute-start(bf16[128,4096]{1,0:T(8,128)(2,1)} %param.31), channel_id=1, source_target_pairs={{7,0},{8,1},{9,2},{10,3},{11,4},{12,5},{13,6},{14,7},{15,8},{23,16... | collective-permute-start | bytes 3145736 | tf_op jit(solution)/shard_map/ppermute | solution.py:15
  186.8 2.0 convert_reduce_fusion.14
  192.2 6.4 %conditional.16 = (f32[128]{0:T(128)S(1)}, f32[128,4096]{1,0:T(8,128)}) conditional(s32[]{:T(128)} %convert_element_type.328, () %tuple.177, (s32[]{:T(128)}, s32[]{:T(128)}, s32[6]{0:T(128)S(1)}, s32[6]{0:T(128)S(1)}, s32[6]{0:T(128)S(1)}, /*index=5*/pred[6]{0:T(512)(128)(4,1)S(1)}, s32[6]{0:T(128)S(1)}, f32[128]{0:T(128)S(1)}, ...), branch_computations={%region_18.19_spmd, %region_19.22_spmd} | conditional | flops 271171872 | bytes 10556090 | solution.py:92
  196.8 1.8 fusion.10
  198.6 6.5 %conditional.17 = (f32[128]{0:T(128)S(1)}, f32[128,4096]{1,0:T(8,128)}) conditional(s32[]{:T(128)} %convert_element_type.329, () %tuple.179, (s32[]{:T(128)}, s32[]{:T(128)}, s32[6]{0:T(128)S(1)}, s32[6]{0:T(128)S(1)}, s32[6]{0:T(128)S(1)}, /*index=5*/pred[6]{0:T(512)(128)(4,1)S(1)}, s32[6]{0:T(128)S(1)}, f32[128]{0:T(128)S(1)}, ...), branch_computations={%region_24.25_spmd, %region_25.28_spmd} | conditional | flops 271171872 | bytes 10556090 | solution.py:92
  203.2 1.9 fusion.15
  205.1 6.1 %conditional.18 = (f32[128]{0:T(128)S(1)}, f32[128,4096]{1,0:T(8,128)S(1)}) conditional(s32[]{:T(128)} %convert_element_type.330, () %tuple.181, (s32[]{:T(128)}, s32[]{:T(128)}, s32[6]{0:T(128)S(1)}, s32[6]{0:T(128)S(1)}, s32[6]{0:T(128)S(1)}, /*index=5*/pred[6]{0:T(512)(128)(4,1)S(1)}, s32[6]{0:T(128)S(1)}, f32[128]{0:T(128)S(1)}, ...), branch_computations={%region_30.31_spmd, %region_31.34_spmd} | conditional | flops 271171872 | bytes 6361758 | solution.py:92
  212.5 6.3 %conditional.19 = (f32[128]{0:T(128)S(1)}, f32[128,4096]{1,0:T(8,128)S(1)}) conditional(s32[]{:T(128)} %convert_element_type.331, () %tuple.183, (s32[]{:T(128)}, s32[]{:T(128)}, s32[6]{0:T(128)S(1)}, s32[6]{0:T(128)S(1)}, s32[6]{0:T(128)S(1)}, /*index=5*/pred[6]{0:T(512)(128)(4,1)S(1)}, s32[6]{0:T(128)S(1)}, f32[128]{0:T(128)S(1)}, ...), branch_computations={%region_36.37_spmd, %region_37.40_spmd} | conditional | flops 271171872 | bytes 6361758 | solution.py:92
  220.1 6.3 %conditional.20 = (f32[128]{0:T(128)S(1)}, f32[128,4096]{1,0:T(8,128)S(1)}) conditional(s32[]{:T(128)} %convert_element_type.332, () %tuple.185, (s32[]{:T(128)}, s32[]{:T(128)}, s32[6]{0:T(128)S(1)}, s32[6]{0:T(128)S(1)}, s32[6]{0:T(128)S(1)}, /*index=5*/pred[6]{0:T(512)(128)(4,1)S(1)}, s32[6]{0:T(128)S(1)}, f32[128]{0:T(128)S(1)}, ...), branch_computations={%region_42.43_spmd, %region_43.46_spmd} | conditional | flops 271171872 | bytes 6361758 | solution.py:92
  227.7 6.1 %conditional.21 = (f32[128]{0:T(128)S(1)}, f32[128,4096]{1,0:T(8,128)S(1)}) conditional(s32[]{:T(128)} %convert_element_type.333, () %tuple.187, (s32[]{:T(128)}, s32[]{:T(128)}, s32[6]{0:T(128)S(1)}, s32[6]{0:T(128)S(1)}, s32[6]{0:T(128)S(1)}, /*index=5*/pred[6]{0:T(512)(128)(4,1)S(1)}, s32[6]{0:T(128)S(1)}, f32[128]{0:T(128)S(1)}, ...), branch_computations={%region_48.49_spmd, %region_49.52_spmd} | conditional | flops 271171872 | bytes 6361758 | solution.py:92
  235.2 6.4 %conditional.22 = (f32[128]{0:T(128)S(1)}, f32[128,4096]{1,0:T(8,128)}) conditional(s32[]{:T(128)} %convert_element_type.334, () %tuple.189, (s32[]{:T(128)}, s32[]{:T(128)}, s32[6]{0:T(128)S(1)}, s32[6]{0:T(128)S(1)}, s32[6]{0:T(128)S(1)}, /*index=5*/pred[6]{0:T(512)(128)(4,1)S(1)}, s32[6]{0:T(128)S(1)}, f32[128]{0:T(128)S(1)}, ...), branch_computations={%region_54.55_spmd, %region_55.58_spmd} | conditional | flops 271171872 | bytes 10556090 | solution.py:92
  243.4 26.0 %collective-permute-done.11 = bf16[128,4096]{1,0:T(8,128)(2,1)} collective-permute-done((bf16[128,4096]{1,0:T(8,128)(2,1)}, bf16[128,4096]{1,0:T(8,128)(2,1)}, u32[]{:S(2)}, u32[]{:S(2)}) %collective-permute-start.11) | collective-permute-done | bytes 1048608 | tf_op jit(solution)/shard_map/ppermute | solution.py:15
  269.6 21.7 %collective-permute-done.12 = bf16[128,4096]{1,0:T(8,128)(2,1)} collective-permute-done((bf16[128,4096]{1,0:T(8,128)(2,1)}, bf16[128,4096]{1,0:T(8,128)(2,1)}, u32[]{:S(2)}, u32[]{:S(2)}) %collective-permute-start.12) | collective-permute-done | bytes 1048608 | tf_op jit(solution)/shard_map/ppermute | solution.py:15
  293.1 9.4 %collective-permute-done.13 = bf16[128,4096]{1,0:T(8,128)(2,1)S(1)} collective-permute-done((bf16[128,4096]{1,0:T(8,128)(2,1)}, bf16[128,4096]{1,0:T(8,128)(2,1)S(1)}, u32[]{:S(2)}, u32[]{:S(2)}) %collective-permute-start.13) | collective-permute-done | bytes 1048608 | tf_op jit(solution)/shard_map/ppermute | solution.py:15
  304.1 12.3 %select_convert_fusion = bf16[128,4096]{1,0:T(8,128)(2,1)} fusion(f32[128,4096]{1,0:T(8,128)} %get-tuple-element.984, f32[128,4096]{1,0:T(8,128)} %copy-done.18, f32[128,4096]{1,0:T(8,128)} %copy-done.17, f32[128,4096]{1,0:T(8,128)} %copy-done.16, f32[128,4096]{1,0:T(8,128)} %copy-done.15, f32[128,4096]{1,0:T(8,128)} %get-tuple-element.979, ...), kind=kLoop, calls=%fused_computation.200 | loop fusion | flops 8912896 | bytes 32506496 | tf_op jit(solution)/shard_map/convert_element_type | solution.py:98
  (129 shorter events, 70.6 us)
Async XLA Ops:
  0.0 188.9 %copy-start = (bf16[128,4096]{1,0:T(8,128)(2,1)S(1)}, bf16[128,4096]{1,0:T(8,128)(2,1)}, u32[]{:S(2)}) copy-start(bf16[128,4096]{1,0:T(8,128)(2,1)} %param.31) | copy-start | bytes 3145732
  0.0 28.1 %collective-permute-start.1 = (bf16[128,4096]{1,0:T(8,128)(2,1)}, bf16[128,4096]{1,0:T(8,128)(2,1)S(1)}, u32[]{:S(2)}, u32[]{:S(2)}) collective-permute-start(bf16[128,4096]{1,0:T(8,128)(2,1)} %param.31), channel_id=1, source_target_pairs={{0,6},{1,7},{2,8},{3,9},{4,10},{5,11},{6,12},{7,13},{8,14},{9,15},... | collective-permute-start | bytes 3145736 | tf_op jit(solution)/shard_map/ppermute | solution.py:15
  4.3 47.4 %collective-permute-start.2 = (bf16[128,4096]{1,0:T(8,128)(2,1)}, bf16[128,4096]{1,0:T(8,128)(2,1)S(1)}, u32[]{:S(2)}, u32[]{:S(2)}) collective-permute-start(bf16[128,4096]{1,0:T(8,128)(2,1)} %param.31), channel_id=1, source_target_pairs={{0,5},{1,6},{2,7},{3,8},{4,9},{5,10},{6,11},{7,12},{8,13},{9,14},{... | collective-permute-start | bytes 3145736 | tf_op jit(solution)/shard_map/ppermute | solution.py:15
  6.2 66.0 %collective-permute-start.3 = (bf16[128,4096]{1,0:T(8,128)(2,1)}, bf16[128,4096]{1,0:T(8,128)(2,1)S(1)}, u32[]{:S(2)}, u32[]{:S(2)}) collective-permute-start(bf16[128,4096]{1,0:T(8,128)(2,1)} %param.31), channel_id=1, source_target_pairs={{0,4},{1,5},{2,6},{3,7},{4,8},{5,9},{6,10},{7,11},{8,12},{9,13},{1... | collective-permute-start | bytes 3145736 | tf_op jit(solution)/shard_map/ppermute | solution.py:15
  8.2 122.2 %collective-permute-start.4 = (bf16[128,4096]{1,0:T(8,128)(2,1)}, bf16[128,4096]{1,0:T(8,128)(2,1)}, u32[]{:S(2)}, u32[]{:S(2)}) collective-permute-start(bf16[128,4096]{1,0:T(8,128)(2,1)} %param.31), channel_id=1, source_target_pairs={{0,3},{1,4},{2,5},{3,6},{4,7},{5,8},{6,9},{7,10},{8,11},{9,12},{10... | collective-permute-start | bytes 3145736 | tf_op jit(solution)/shard_map/ppermute | solution.py:15
  10.1 155.4 %collective-permute-start.5 = (bf16[128,4096]{1,0:T(8,128)(2,1)}, bf16[128,4096]{1,0:T(8,128)(2,1)}, u32[]{:S(2)}, u32[]{:S(2)}) collective-permute-start(bf16[128,4096]{1,0:T(8,128)(2,1)} %param.31), channel_id=1, source_target_pairs={{0,2},{1,3},{2,4},{3,5},{4,6},{5,7},{6,8},{7,9},{8,10},{9,11},{10,... | collective-permute-start | bytes 3145736 | tf_op jit(solution)/shard_map/ppermute | solution.py:15
  28.1 104.2 %copy-start.7 = (bf16[128,4096]{1,0:T(8,128)(2,1)}, bf16[128,4096]{1,0:T(8,128)(2,1)S(1)}, u32[]{:S(2)}) copy-start(bf16[128,4096]{1,0:T(8,128)(2,1)S(1)} %collective-permute-done.1) | copy-start | bytes 3145732
  28.1 139.3 %collective-permute-start.6 = (bf16[128,4096]{1,0:T(8,128)(2,1)}, bf16[128,4096]{1,0:T(8,128)(2,1)}, u32[]{:S(2)}, u32[]{:S(2)}) collective-permute-start(bf16[128,4096]{1,0:T(8,128)(2,1)} %param.31), channel_id=1, source_target_pairs={{0,1},{1,2},{2,3},{3,4},{4,5},{5,6},{6,7},{7,8},{8,9},{9,10},{10,1... | collective-permute-start | bytes 3145736 | tf_op jit(solution)/shard_map/ppermute | solution.py:15
  51.7 78.6 %copy-start.5 = (bf16[128,4096]{1,0:T(8,128)(2,1)}, bf16[128,4096]{1,0:T(8,128)(2,1)S(1)}, u32[]{:S(2)}) copy-start(bf16[128,4096]{1,0:T(8,128)(2,1)S(1)} %collective-permute-done.2) | copy-start | bytes 3145732
  51.7 117.6 %collective-permute-start.7 = (bf16[128,4096]{1,0:T(8,128)(2,1)}, bf16[128,4096]{1,0:T(8,128)(2,1)}, u32[]{:S(2)}, u32[]{:S(2)}) collective-permute-start(bf16[128,4096]{1,0:T(8,128)(2,1)} %param.31), channel_id=1, source_target_pairs={{1,0},{2,1},{3,2},{4,3},{5,4},{6,5},{7,6},{8,7},{9,8},{10,9},{11,1... | collective-permute-start | bytes 3145736 | tf_op jit(solution)/shard_map/ppermute | solution.py:15
  72.2 36.9 %copy-start.3 = (bf16[128,4096]{1,0:T(8,128)(2,1)}, bf16[128,4096]{1,0:T(8,128)(2,1)S(1)}, u32[]{:S(2)}) copy-start(bf16[128,4096]{1,0:T(8,128)(2,1)S(1)} %collective-permute-done.3) | copy-start | bytes 3145732
  72.2 104.7 %collective-permute-start.8 = (bf16[128,4096]{1,0:T(8,128)(2,1)}, bf16[128,4096]{1,0:T(8,128)(2,1)S(1)}, u32[]{:S(2)}, u32[]{:S(2)}) collective-permute-start(bf16[128,4096]{1,0:T(8,128)(2,1)} %param.31), channel_id=1, source_target_pairs={{2,0},{3,1},{4,2},{5,3},{6,4},{7,5},{8,6},{9,7},{10,8},{11,9},{12,... | collective-permute-start | bytes 3145736 | tf_op jit(solution)/shard_map/ppermute | solution.py:15
  130.4 47.8 %collective-permute-start.9 = (bf16[128,4096]{1,0:T(8,128)(2,1)}, bf16[128,4096]{1,0:T(8,128)(2,1)S(1)}, u32[]{:S(2)}, u32[]{:S(2)}) collective-permute-start(bf16[128,4096]{1,0:T(8,128)(2,1)} %param.31), channel_id=1, source_target_pairs={{3,0},{4,1},{5,2},{6,3},{7,4},{8,5},{9,6},{10,7},{11,8},{12,9},{13... | collective-permute-start | bytes 3145736 | tf_op jit(solution)/shard_map/ppermute | solution.py:15
  165.5 76.4 %collective-permute-start.10 = (bf16[128,4096]{1,0:T(8,128)(2,1)}, bf16[128,4096]{1,0:T(8,128)(2,1)}, u32[]{:S(2)}, u32[]{:S(2)}) collective-permute-start(bf16[128,4096]{1,0:T(8,128)(2,1)} %param.31), channel_id=1, source_target_pairs={{4,0},{5,1},{6,2},{7,3},{8,4},{9,5},{10,6},{11,7},{12,8},{13,9},{1... | collective-permute-start | bytes 3145736 | tf_op jit(solution)/shard_map/ppermute | solution.py:15
  167.4 102.0 %collective-permute-start.11 = (bf16[128,4096]{1,0:T(8,128)(2,1)}, bf16[128,4096]{1,0:T(8,128)(2,1)}, u32[]{:S(2)}, u32[]{:S(2)}) collective-permute-start(bf16[128,4096]{1,0:T(8,128)(2,1)} %param.31), channel_id=1, source_target_pairs={{5,0},{6,1},{7,2},{8,3},{9,4},{10,5},{11,6},{12,7},{13,8},{14,9},{... | collective-permute-start | bytes 3145736 | tf_op jit(solution)/shard_map/ppermute | solution.py:15
  169.3 121.9 %collective-permute-start.12 = (bf16[128,4096]{1,0:T(8,128)(2,1)}, bf16[128,4096]{1,0:T(8,128)(2,1)}, u32[]{:S(2)}, u32[]{:S(2)}) collective-permute-start(bf16[128,4096]{1,0:T(8,128)(2,1)} %param.31), channel_id=1, source_target_pairs={{6,0},{7,1},{8,2},{9,3},{10,4},{11,5},{12,6},{13,7},{14,8},{15,9},... | collective-permute-start | bytes 3145736 | tf_op jit(solution)/shard_map/ppermute | solution.py:15
  176.9 1.3 copy-start.1
  176.9 114.6 %collective-permute-start = (bf16[128,4096]{1,0:T(8,128)(2,1)}, bf16[128,4096]{1,0:T(8,128)(2,1)}, u32[]{:S(2)}, u32[]{:S(2)}) collective-permute-start(bf16[128,4096]{1,0:T(8,128)(2,1)} %param.31), channel_id=1, source_target_pairs={{0,7},{1,8},{2,9},{3,10},{4,11},{5,12},{6,13},{7,14},{8,15},{16,23... | collective-permute-start | bytes 3145736 | tf_op jit(solution)/shard_map/ppermute | solution.py:15
  178.2 124.3 %collective-permute-start.13 = (bf16[128,4096]{1,0:T(8,128)(2,1)}, bf16[128,4096]{1,0:T(8,128)(2,1)S(1)}, u32[]{:S(2)}, u32[]{:S(2)}) collective-permute-start(bf16[128,4096]{1,0:T(8,128)(2,1)} %param.31), channel_id=1, source_target_pairs={{7,0},{8,1},{9,2},{10,3},{11,4},{12,5},{13,6},{14,7},{15,8},{23,16... | collective-permute-start | bytes 3145736 | tf_op jit(solution)/shard_map/ppermute | solution.py:15
  188.8 1.8 copy-start.8
  195.0 1.8 copy-start.6
  201.4 1.8 copy-start.4
  211.2 1.3 copy-start.11
  218.7 1.3 copy-start.12
  226.4 1.3 copy-start.13
  233.8 1.4 copy-start.14
  238.0 1.8 copy-start.2
  241.8 1.3 copy-start.15
  243.3 26.0 %copy-start.16 = (f32[128,4096]{1,0:T(8,128)}, f32[128,4096]{1,0:T(8,128)S(1)}, u32[]{:S(2)}) copy-start(f32[128,4096]{1,0:T(8,128)S(1)} %get-tuple-element.981) | copy-start | bytes 6291460
  269.6 21.7 %copy-start.17 = (f32[128,4096]{1,0:T(8,128)}, f32[128,4096]{1,0:T(8,128)S(1)}, u32[]{:S(2)}) copy-start(f32[128,4096]{1,0:T(8,128)S(1)} %get-tuple-element.982) | copy-start | bytes 6291460
  291.5 1.4 copy-start.18
  293.1 9.4 %copy-start.19 = (f32[128,4096]{1,0:T(8,128)}, f32[128,4096]{1,0:T(8,128)S(1)}, u32[]{:S(2)}) copy-start(f32[128,4096]{1,0:T(8,128)S(1)} %get-tuple-element.971) | copy-start | bytes 6291460
where the time goes:
time: 321 us; the launch traced here: 317 us
  waiting for transfers between devices  137 us (43%)
  starting transfers between devices  71.7 us (22%)
  other arithmetic  42.8 us (13%)
  matrix products  28.1 us (9%)
  between operations  19.9 us (6%)
  local copies, waits for them, and re-layouts  12.1 us (4%)
  loops' own time  4.5 us (1%)
    ppermute x14, waiting for transfers between devices, shifted(): lax.ppermute(value, axis, [(source, source + steps) for source in range(f...  137 us
    ppermute x14, starting transfers between devices, shifted(): lax.ppermute(value, axis, [(source, source + steps) for source in range(f...  71.7 us
    dot_general x8, matrix products, pair_weights(): lax.dot_general(own_block, other_block, (((1,), (1,)), ((), ())), preferr...  14.1 us
    convert_element_type x1, other arithmetic, body(): return result.astype(jnp.bfloat16)  12.3 us
    dot_general x7, matrix products, compute_pair(): jnp.dot(weights, other_block, preferred_element_type=jnp.float32)  12.2 us
    dot_general x8, other arithmetic, inverse_norms(): jnp.einsum('ij,ij->i', block, block, preferred_element_type=jnp.float32)  12.1 us
    reduce_or x15, other arithmetic, tile_layout(): present = jnp.any(inside)  9.92 us
    unnamed x30, local copies, waits for them, and re-layouts  7.98 us
  transfers between devices with their start and end apart: 14, of which 8 were waited for; matrix products, arithmetic and copies ran while one was open for 19% of the time, Pallas kernels for 0%

commit v1 on v0

v1 whole, which is shorter than its diff:
```python
import functools

import jax
import jax.numpy as jnp
from jax import lax
from jax.experimental import pallas as pl
from jax.experimental.pallas import tpu as pltpu
from jax.sharding import PartitionSpec as P

MOST = 8
TILE = 128
HALF = 64

similarity_scale = 64.0


def across(row, column, core):
    return row, 1 - column


def along(row, column, core):
    return row + 2 * column - 1, column


def against(row, column, core):
    return row + 1 - 2 * column, column


def far_along(row, column, core):
    return along(row, column, core) if core == column else None


def far_against(row, column, core):
    return against(row, column, core) if core != column else None


STEPS = (
    ("a0", "0", along),
    ("y", "e", across),
    ("b", "e", against),
    ("a1", "1", along),
    ("w0", "a0", across),
    ("w1", "a1", across),
    ("b2", "b", far_against),
    ("x", "y", along),
    ("r0", "w0", against),
    ("r1", "w1", against),
    ("a20", "a0", far_along),
    ("a21", "a1", far_along),
)


def routes(tiles):
    held = {value: [2 * d + (value == "1") for d in range(tiles)] for value in ("0", "1", "e")}
    sizes = {"0": HALF, "1": HALF, "e": TILE}
    pairs, rows, table = [], [], []
    for name, value, direction in STEPS:
        landed, moves = [-1] * tiles, []
        for source in range(tiles):
            target = direction(source // 4, source // 2 % 2, source % 2)
            if target is None or not 0 <= target[0] < tiles // 4 or held[value][source] < 0:
                continue
            place = 4 * target[0] + 2 * target[1] + source % 2
            moves.append((source, place))
            landed[place] = held[value][source]
        held[name], sizes[name] = landed, sizes[value]
        pairs.append(tuple(moves))
        rows.append(sizes[value])
        table.append(landed)
    for device in range(tiles):
        got = []
        for landed, count in zip(table, rows):
            if landed[device] >= 0:
                got += [landed[device]] if count == HALF else [landed[device], landed[device] + 1]
        assert len(got) == len(set(got))
        for tile in (device, device ^ 1):
            for far in range(max(0, tile - MOST + 1), min(tiles, tile + MOST)):
                if far % 2 == device % 2 and far != device:
                    assert {2 * far, 2 * far + 1} <= set(got), (device, far)
    return pairs, rows, table


def attend_kernel(rows, units, clusters, tiles_ref, pad_ref, table_ref, own_ref, sib_ref, *rest):
    pieces = rest[: len(rows)]
    own_out, sib_out, held, weights, limits, den, sems = rest[len(rows) :]
    width = own_ref.shape[1]
    me = lax.axis_index("tiles")
    other = me + 1 - 2 * lax.rem(me, 2)

    def layout(tile):
        start, cluster, live = jnp.int32(0), jnp.int32(-1), jnp.int32(0)
        for c in range(clusters):
            count = tiles_ref[c]
            inside = (start <= tile) & (tile < start + count)
            cluster = jnp.where(inside, c, cluster)
            live = jnp.where(inside, count * TILE - pad_ref[c] - (tile - start) * TILE, live)
            start = start + count
        return cluster, jnp.clip(live, 0, TILE)

    copies = [
        pltpu.make_async_copy(sib_ref, held.at[pl.ds(0, TILE)], sems.at[0]),
        pltpu.make_async_copy(own_ref, held.at[pl.ds(TILE, TILE)], sems.at[1]),
    ]
    for copy in copies:
        copy.start()
    own_cluster, own_live = layout(me)
    sib_cluster, sib_live = layout(other)

    def note(unit, cluster, live):
        limits[0, unit] = jnp.where(cluster == own_cluster, jnp.clip(live, 0, HALF), 0)
        limits[1, unit] = jnp.where(cluster == sib_cluster, jnp.clip(live, 0, HALF), 0)

    note(0, own_cluster, own_live)
    note(1, own_cluster, own_live - HALF)

    used = jnp.int32(2)
    pending = []
    for i, count in enumerate(rows):
        piece = table_ref[me * len(rows) + i]
        cluster, live = layout(lax.shift_right_arithmetic(piece, 1))
        live = live - HALF * (piece & 1)
        valid = (piece >= 0) & ((cluster == own_cluster) | (cluster == sib_cluster))
        place = pl.multiple_of(TILE + used * HALF, HALF)
        copy = pltpu.make_async_copy(pieces[i], held.at[pl.ds(place, count)], sems.at[2 + i])

        @pl.when(valid)
        def _(copy=copy, used=used, cluster=cluster, live=live, count=count):
            copy.start()
            note(used, cluster, live)
            if count == TILE:
                note(used + 1, cluster, live - HALF)

        pending.append((valid, copy))
        used = used + jnp.where(valid, count // HALF, 0)

    few = used <= units // 2
    bound = jnp.where(few, units // 2, units)
    for unit in range(2, units):

        @pl.when((unit >= used) & (unit < bound))
        def _(unit=unit):
            held[pl.ds(TILE + unit * HALF, HALF), :] = jnp.zeros((HALF, width), held.dtype)
            limits[0, unit] = jnp.int32(0)
            limits[1, unit] = jnp.int32(0)

    for copy in copies:
        copy.wait()
    for valid, copy in pending:

        @pl.when(valid)
        def _(copy=copy):
            copy.wait()

    def inverse(block):
        wide = block.astype(jnp.float32)
        return lax.rsqrt(jnp.sum(wide * wide, axis=1, keepdims=True) + 1e-06)

    inv_rows = jnp.concatenate([inverse(held[pl.ds(0, TILE), :]), inverse(held[pl.ds(TILE, TILE), :])], axis=0)
    den[...] = jnp.zeros_like(den)
    row = lax.broadcasted_iota(jnp.int32, (2 * TILE, TILE), 0)
    lane = lax.broadcasted_iota(jnp.int32, (2 * TILE, TILE), 1)
    is_sib = row < TILE
    row_live = row < jnp.where(is_sib, sib_live, own_live + TILE)

    @pl.loop(0, bound // 2)
    def _(b):
        columns = held[pl.ds(pl.multiple_of(TILE + b * TILE, TILE), TILE), :]
        gram = lax.dot_general(
            held[pl.ds(0, 2 * TILE), :], columns, (((1,), (1,)), ((), ())), preferred_element_type=jnp.float32
        )
        inv_columns = jnp.broadcast_to(inverse(columns), (TILE, TILE)).T[0:1, :]
        scores = similarity_scale * inv_rows * inv_columns * gram
        low = jnp.where(is_sib, limits[1, 2 * b], limits[0, 2 * b])
        high = jnp.where(is_sib, limits[1, 2 * b + 1], limits[0, 2 * b + 1])
        keep = row_live & (lane < jnp.where(lane < HALF, low, high + HALF))
        keep = keep & ((row - TILE != lane) | (b != 0))
        block = jnp.where(keep, jnp.exp(scores), 0.0).astype(jnp.bfloat16)
        weights[:, pl.ds(pl.multiple_of(b * TILE, TILE), TILE)] = block
        den[...] += jnp.broadcast_to(jnp.sum(block.astype(jnp.float32), axis=1, keepdims=True), den.shape)

    chunk = 512

    def products(depth):
        @pl.loop(0, width // chunk)
        def _(f):
            at = pl.ds(pl.multiple_of(f * chunk, chunk), chunk)
            total = jnp.dot(
                weights[:, pl.ds(0, depth)], held[pl.ds(TILE, depth), at], preferred_element_type=jnp.float32
            )
            sib_out[:, at] = total[:TILE].astype(jnp.bfloat16)
            own_out[:, at] = total[TILE:]

    @pl.when(few)
    def _():
        products(units // 2 * HALF)

    @pl.when(jnp.logical_not(few))
    def _():
        products(units * HALF)

    own_out[:, pl.ds(width, TILE)] = den[pl.ds(TILE, TILE), :]
    whole = den[pl.ds(0, TILE), :]
    first = whole.astype(jnp.bfloat16).astype(jnp.float32)
    second = (whole - first).astype(jnp.bfloat16).astype(jnp.float32)
    third = whole - first - second
    part = lax.broadcasted_iota(jnp.int32, (TILE, TILE), 1)
    sib_out[:, pl.ds(width, TILE)] = jnp.where(
        part == 0, first, jnp.where(part == 1, second, jnp.where(part == 2, third, 0.0))
    ).astype(jnp.bfloat16)


def attend(tiles, routed, cluster_tiles, last_tile_pad, own, sibling, pieces):
    _, rows, table = routed
    units = 2 * MOST
    width = own.shape[1]
    flat = jnp.array([landed[d] for d in range(tiles) for landed in table], jnp.int32)
    smem = pl.BlockSpec(memory_space=pltpu.SMEM)
    anywhere = pl.BlockSpec(memory_space=pl.ANY)
    vmem = pl.BlockSpec(memory_space=pltpu.VMEM)
    return pl.pallas_call(
        functools.partial(attend_kernel, tuple(rows), units, cluster_tiles.shape[0]),
        out_shape=(
            jax.ShapeDtypeStruct((TILE, width + TILE), jnp.float32),
            jax.ShapeDtypeStruct((TILE, width + TILE), jnp.bfloat16),
        ),
        in_specs=[smem] * 3 + [anywhere] * (2 + len(rows)),
        out_specs=(vmem, vmem),
        scratch_shapes=[
            pltpu.VMEM((TILE + units * HALF, width), jnp.bfloat16),
            pltpu.VMEM((2 * TILE, units * HALF), jnp.bfloat16),
            pltpu.SMEM((2, units), jnp.int32),
            pltpu.VMEM((2 * TILE, TILE), jnp.float32),
            pltpu.SemaphoreType.DMA((2 + len(rows),)),
        ],
        compiler_params=pltpu.CompilerParams(vmem_limit_bytes=32 * 1024 * 1024),
    )(cluster_tiles, last_tile_pad, flat, own, sibling, *pieces)


def body(embeddings, cluster_tiles, last_tile_pad):
    width = embeddings.shape[1]
    tiles = lax.axis_size("tiles")
    routed = routes(tiles)
    cores = [(i, i ^ 1) for i in range(tiles)]
    held = {"0": embeddings[:HALF], "1": embeddings[HALF:], "e": embeddings}
    for (name, value, _), pairs in zip(STEPS, routed[0]):
        held[name] = lax.ppermute(held[value], "tiles", pairs)
    sibling = lax.ppermute(embeddings, "tiles", cores)
    pieces = [held[name] for name, _, _ in STEPS]
    own_sum, sib_sum = attend(tiles, routed, cluster_tiles, last_tile_pad, embeddings, sibling, pieces)
    other_sum = lax.ppermute(sib_sum, "tiles", cores)
    numer = own_sum[:, :width] + other_sum[:, :width].astype(jnp.float32)
    parts = other_sum[:, width : width + 3].astype(jnp.float32)
    denom = own_sum[:, width] + (parts[:, 0] + parts[:, 1] + parts[:, 2])
    live = denom > 0.0
    return jnp.where(live[:, None], numer / jnp.where(live, denom, 1.0)[:, None], 0.0).astype(jnp.bfloat16)


def solution(mesh):
    placed = (P(("groups", "tiles"), None), P("groups"), P("groups"))
    return jax.shard_map(
        body, mesh=mesh, in_specs=placed, out_specs=P(("groups", "tiles"), None), check_vma=False
    )
```

time: 321 us -> 100 us (0.31); the launches traced: 317 us -> 99.8 us
  waiting for transfers between devices: 137 us -> 53.5 us
  other arithmetic: 42.8 us -> 1.68 us
  starting transfers between devices: 71.7 us -> 30.6 us
  matrix products: 28.1 us -> 0 us
  between operations: 19.9 us -> 0.19 us
  Pallas kernels: 0 us -> 12.4 us
  local copies, waits for them, and re-layouts: 12.1 us -> 1.37 us
  loops' own time: 4.5 us -> 0 us
    ppermute x14, waiting for transfers between devices: 137 us -> 53.5 us  [the longest x12 50.8 us: body(): held[name] = lax.ppermute(held[value], 'tiles', pairs)]
    ppermute x14, starting transfers between devices: 71.7 us -> 30.6 us  [the longest x12 29 us: body(): held[name] = lax.ppermute(held[value], 'tiles', pairs)]
    dot_general x16 -> x0, matrix products: 28.1 us -> none  [the longest x8 14.1 us: pair_weights(): lax.dot_general(own_block, other_block, (((1,), (1,)), ((), ())), preferr...]
    pallas_call x0 -> x1, Pallas kernels: none -> 12.4 us  [attend(): pl.pallas_call(functools.partial(attend_kernel, tuple(rows), units, clust...]
    dot_general x8 -> x0, other arithmetic: 12.1 us -> none  [inverse_norms(): jnp.einsum('ij,ij->i', block, block, preferred_element_type=jnp.float32)]
    convert_element_type x1 -> x2, other arithmetic: 12.3 us -> 1.39 us  [the longest x1 1.38 us: body(): jnp.where(live[:, None], numer / jnp.where(live, denom, 1.0)[:, None], 0.0)]
    reduce_or x15 -> x0, other arithmetic: 9.92 us -> none  [tile_layout(): present = jnp.any(inside)]
    unnamed x30 -> x8, local copies, waits for them, and re-layouts: 7.98 us -> 0.02 us
  transfers between devices with their start and end apart: 14 -> 14, of which waited for: 8 -> 7; matrix products, arithmetic and copies ran while one was open for 19% -> 0% of each run, Pallas kernels for 0% -> 0%
where the time goes in v1:
time: 100 us; the launch traced here: 99.8 us
  waiting for transfers between devices  53.5 us (54%)
  starting transfers between devices  30.6 us (31%)
  Pallas kernels  12.4 us (12%)
  other arithmetic  1.68 us (2%)
  local copies, waits for them, and re-layouts  1.37 us (1%)
    ppermute x12, waiting for transfers between devices, body(): held[name] = lax.ppermute(held[value], 'tiles', pairs)  50.8 us
    ppermute x12, starting transfers between devices, body(): held[name] = lax.ppermute(held[value], 'tiles', pairs)  29 us
    pallas_call x1, Pallas kernels, attend(): pl.pallas_call(functools.partial(attend_kernel, tuple(rows), units, clust...  12.4 us
    ppermute x1, waiting for transfers between devices, body(): other_sum = lax.ppermute(sib_sum, 'tiles', cores)  2.69 us
  transfers between devices with their start and end apart: 14, of which 7 were waited for; matrix products, arithmetic and copies ran while one was open for 0% of the time, Pallas kernels for 0%

profile of v1, /device:TPU:17, one launch (start us, length us, event | category | flops | bytes accessed | tf_op | source)
XLA Modules:
  0.0 99.8 jit_solution(6674743740679935497)
XLA Ops:
  0.0 1.4 %fusion.3 = (bf16[64,4096]{1,0:T(8,128)(2,1)S(1)}, bf16[64,4096]{1,0:T(8,128)(2,1)S(1)}) fusion(bf16[128,4096]{1,0:T(8,128)(2,1)} %own_ref.1), kind=kLoop, calls=%fused_computation.8 | loop fusion | bytes 2097152 | tf_op jit(solution)/shard_map/slice | solution.py:244
  1.4 2.1 %collective-permute-start.4 = (bf16[64,4096]{1,0:T(8,128)(2,1)S(1)}, bf16[64,4096]{1,0:T(8,128)(2,1)S(1)}, u32[]{:S(2)}, u32[]{:S(2)}) collective-permute-start(bf16[64,4096]{1,0:T(8,128)(2,1)S(1)} %get-tuple-element.11), channel_id=1, source_target_pairs={{2,6},{3,7},{4,0},{5,1},{6,10},{7,11},{8,4},{9,5},{10,14},{11,15},... | collective-permute-start | bytes 1572872 | tf_op jit(solution)/shard_map/ppermute | solution.py:246
  3.5 2.4 %collective-permute-start.2 = (bf16[128,4096]{1,0:T(8,128)(2,1)S(1)}, bf16[128,4096]{1,0:T(8,128)(2,1)S(1)}, u32[]{:S(2)}, u32[]{:S(2)}) collective-permute-start(bf16[128,4096]{1,0:T(8,128)(2,1)S(1)} %copy-done), channel_id=1, source_target_pairs={{0,2},{1,3},{2,0},{3,1},{4,6},{5,7},{6,4},{7,5},{8,10},{9,11},{10,... | collective-permute-start | bytes 3145736 | tf_op jit(solution)/shard_map/ppermute | solution.py:246
  5.9 1.9 %collective-permute-start.3 = (bf16[128,4096]{1,0:T(8,128)(2,1)S(1)}, bf16[128,4096]{1,0:T(8,128)(2,1)S(1)}, u32[]{:S(2)}, u32[]{:S(2)}) collective-permute-start(bf16[128,4096]{1,0:T(8,128)(2,1)S(1)} %copy-done), channel_id=1, source_target_pairs={{0,4},{1,5},{4,8},{5,9},{6,2},{7,3},{8,12},{9,13},{10,6},{11,7},{1... | collective-permute-start | bytes 3145736 | tf_op jit(solution)/shard_map/ppermute | solution.py:246
  7.8 3.4 %collective-permute-start.1 = (bf16[64,4096]{1,0:T(8,128)(2,1)S(1)}, bf16[64,4096]{1,0:T(8,128)(2,1)S(1)}, u32[]{:S(2)}, u32[]{:S(2)}) collective-permute-start(bf16[64,4096]{1,0:T(8,128)(2,1)S(1)} %get-tuple-element.12), channel_id=1, source_target_pairs={{2,6},{3,7},{4,0},{5,1},{6,10},{7,11},{8,4},{9,5},{10,14},{11,15},... | collective-permute-start | bytes 1572872 | tf_op jit(solution)/shard_map/ppermute | solution.py:246
  11.2 4.9 %collective-permute-done.4.rest_3_ = bf16[64,4096]{1,0:T(8,128)(2,1)S(1)} collective-permute-done((bf16[64,4096]{1,0:T(8,128)(2,1)S(1)}, bf16[64,4096]{1,0:T(8,128)(2,1)S(1)}, u32[]{:S(2)}, u32[]{:S(2)}) %collective-permute-start.4) | collective-permute-done | bytes 524320 | tf_op jit(solution)/shard_map/ppermute | solution.py:246
  16.1 0.7 collective-permute-start.12
  16.8 5.7 %collective-permute-start.6 = (bf16[64,4096]{1,0:T(8,128)(2,1)S(1)}, bf16[64,4096]{1,0:T(8,128)(2,1)S(1)}, u32[]{:S(2)}, u32[]{:S(2)}) collective-permute-start(bf16[64,4096]{1,0:T(8,128)(2,1)S(1)} %collective-permute-done.4.rest_3_), channel_id=1, source_target_pairs={{0,2},{1,3},{4,6},{5,7},{6,4},{7,5},{8,10},{9,11},{10,8},{11,9},{1... | collective-permute-start | bytes 1572872 | tf_op jit(solution)/shard_map/ppermute | solution.py:246
  22.4 4.9 %collective-permute-done.1.rest_0_ = bf16[64,4096]{1,0:T(8,128)(2,1)S(1)} collective-permute-done((bf16[64,4096]{1,0:T(8,128)(2,1)S(1)}, bf16[64,4096]{1,0:T(8,128)(2,1)S(1)}, u32[]{:S(2)}, u32[]{:S(2)}) %collective-permute-start.1) | collective-permute-done | bytes 524320 | tf_op jit(solution)/shard_map/ppermute | solution.py:246
  27.3 1.5 %collective-permute-start = (bf16[128,4096]{1,0:T(8,128)(2,1)S(1)}, bf16[128,4096]{1,0:T(8,128)(2,1)S(1)}, u32[]{:S(2)}, u32[]{:S(2)}) collective-permute-start(bf16[128,4096]{1,0:T(8,128)(2,1)S(1)} %copy-done), channel_id=1, source_target_pairs={{0,1},{1,0},{2,3},{3,2},{4,5},{5,4},{6,7},{7,6},{8,9},{9,8},{10,11... | collective-permute-start | bytes 3145736 | tf_op jit(solution)/shard_map/ppermute | solution.py:247
  28.9 0.0 collective-permute-done.12.rest_11_
  28.9 0.7 collective-permute-start.11
  29.5 10.2 %collective-permute-done.6.rest_5_ = bf16[64,4096]{1,0:T(8,128)(2,1)S(1)} collective-permute-done((bf16[64,4096]{1,0:T(8,128)(2,1)S(1)}, bf16[64,4096]{1,0:T(8,128)(2,1)S(1)}, u32[]{:S(2)}, u32[]{:S(2)}) %collective-permute-start.6) | collective-permute-done | bytes 524320 | tf_op jit(solution)/shard_map/ppermute | solution.py:246
  39.7 3.0 %collective-permute-start.5 = (bf16[64,4096]{1,0:T(8,128)(2,1)S(1)}, bf16[64,4096]{1,0:T(8,128)(2,1)S(1)}, u32[]{:S(2)}, u32[]{:S(2)}) collective-permute-start(bf16[64,4096]{1,0:T(8,128)(2,1)S(1)} %collective-permute-done.1.rest_0_), channel_id=1, source_target_pairs={{0,2},{1,3},{4,6},{5,7},{6,4},{7,5},{8,10},{9,11},{10,8},{11,9},{1... | collective-permute-start | bytes 1572872 | tf_op jit(solution)/shard_map/ppermute | solution.py:246
  42.8 0.0 collective-permute-done.2.rest_1_
  42.8 2.1 %collective-permute-start.8 = (bf16[128,4096]{1,0:T(8,128)(2,1)S(1)}, bf16[128,4096]{1,0:T(8,128)(2,1)S(1)}, u32[]{:S(2)}, u32[]{:S(2)}) collective-permute-start(bf16[128,4096]{1,0:T(8,128)(2,1)S(1)} %collective-permute-done.2.rest_1_), channel_id=1, source_target_pairs={{2,6},{3,7},{4,0},{5,1},{6,10},{7,11},{8,4},{9,5},{10,14},{11,15},... | collective-permute-start | bytes 3145736 | tf_op jit(solution)/shard_map/ppermute | solution.py:246
  44.9 0.0 collective-permute-done.3.rest_2_
  44.9 3.3 %collective-permute-start.7 = (bf16[128,4096]{1,0:T(8,128)(2,1)S(1)}, bf16[128,4096]{1,0:T(8,128)(2,1)S(1)}, u32[]{:S(2)}, u32[]{:S(2)}) collective-permute-start(bf16[128,4096]{1,0:T(8,128)(2,1)S(1)} %collective-permute-done.3.rest_2_), channel_id=1, source_target_pairs={{5,9},{6,2},{9,13},{10,6},{21,25},{22,18},{25,29},{26,22}} | collective-permute-start | bytes 3145736 | tf_op jit(solution)/shard_map/ppermute | solution.py:246
  48.1 0.0 collective-permute-done.11.rest_10_
  48.2 1.9 %collective-permute-start.10 = (bf16[64,4096]{1,0:T(8,128)(2,1)S(1)}, bf16[64,4096]{1,0:T(8,128)(2,1)S(1)}, u32[]{:S(2)}, u32[]{:S(2)}) collective-permute-start(bf16[64,4096]{1,0:T(8,128)(2,1)S(1)} %collective-permute-done.6.rest_5_), channel_id=1, source_target_pairs={{4,8},{5,9},{6,2},{7,3},{8,12},{9,13},{10,6},{11,7},{20,24},{21,25... | collective-permute-start | bytes 1572872 | tf_op jit(solution)/shard_map/ppermute | solution.py:246
  50.1 3.4 %collective-permute-done.5.rest_4_ = bf16[64,4096]{1,0:T(8,128)(2,1)S(1)} collective-permute-done((bf16[64,4096]{1,0:T(8,128)(2,1)S(1)}, bf16[64,4096]{1,0:T(8,128)(2,1)S(1)}, u32[]{:S(2)}, u32[]{:S(2)}) %collective-permute-start.5) | collective-permute-done | bytes 524320 | tf_op jit(solution)/shard_map/ppermute | solution.py:246
  53.5 1.9 %collective-permute-start.9 = (bf16[64,4096]{1,0:T(8,128)(2,1)S(1)}, bf16[64,4096]{1,0:T(8,128)(2,1)S(1)}, u32[]{:S(2)}, u32[]{:S(2)}) collective-permute-start(bf16[64,4096]{1,0:T(8,128)(2,1)S(1)} %collective-permute-done.5.rest_4_), channel_id=1, source_target_pairs={{4,8},{5,9},{6,2},{7,3},{8,12},{9,13},{10,6},{11,7},{20,24},{21,25... | collective-permute-start | bytes 1572872 | tf_op jit(solution)/shard_map/ppermute | solution.py:246
  55.4 21.9 %collective-permute-done.10.rest_9_ = bf16[64,4096]{1,0:T(8,128)(2,1)S(1)} collective-permute-done((bf16[64,4096]{1,0:T(8,128)(2,1)S(1)}, bf16[64,4096]{1,0:T(8,128)(2,1)S(1)}, u32[]{:S(2)}, u32[]{:S(2)}) %collective-permute-start.10) | collective-permute-done | bytes 524320 | tf_op jit(solution)/shard_map/ppermute | solution.py:246
  77.3 5.6 %collective-permute-done.9.rest_8_ = bf16[64,4096]{1,0:T(8,128)(2,1)S(1)} collective-permute-done((bf16[64,4096]{1,0:T(8,128)(2,1)S(1)}, bf16[64,4096]{1,0:T(8,128)(2,1)S(1)}, u32[]{:S(2)}, u32[]{:S(2)}) %collective-permute-start.9) | collective-permute-done | bytes 524320 | tf_op jit(solution)/shard_map/ppermute | solution.py:246
  82.9 0.0 collective-permute-done.8.rest_7_
  82.9 0.0 collective-permute-done.7.rest_6_
  82.9 12.4 %shard_map.46 = (f32[128,4224]{1,0:T(8,128)S(1)}, bf16[128,4224]{1,0:T(8,128)(2,1)S(1)}) custom-call(s32[6]{0:T(128)S(1)} %copy-done.2, s32[6]{0:T(128)S(1)} %copy-done.3, s32[192]{0:T(256)S(1)} %copy-done.1, bf16[128,4096]{1,0:T(8,128)(2,1)S(1)} %copy-done, bf16[128,4096]{1,0:T(8,128)(2,1)S(1)} %collective-permute-done.sib_ref, ...), custom_call_target="tpu_custom_call" | custom-call | tf_op jit(solution)/shard_map/pallas_call | solution.py:220
  95.3 0.1 collective-permute-start.13
  95.4 2.7 %collective-permute-done.13 = bf16[128,4224]{1,0:T(8,128)(2,1)S(1)} collective-permute-done((bf16[128,4224]{1,0:T(8,128)(2,1)S(1)}, bf16[128,4224]{1,0:T(8,128)(2,1)S(1)}, u32[]{:S(2)}, u32[]{:S(2)}) %collective-permute-start.13) | collective-permute-done | bytes 1081376 | tf_op jit(solution)/shard_map/ppermute | solution.py:250
  98.1 0.2 compare_reduce_fusion
  98.3 0.1 fusion
  98.4 1.4 %select_convert_fusion = bf16[128,4096]{1,0:T(8,128)(2,1)} fusion(f32[128,4224]{1,0:T(8,128)S(1)} %get-tuple-element.7, bf16[128,4224]{1,0:T(8,128)(2,1)S(1)} %collective-permute-done.13, f32[128]{0:T(128)S(1)} %fusion, pred[128]{0:T(512)(128)(4,1)S(1)} %get-tuple-element.9), kind=kLoop, calls=%fused_computation | loop fusion | flops 2621440 | bytes 4194944 | tf_op jit(solution)/shard_map/convert_element_type | solution.py:255
  (10 shorter events, 0.0 us)
Async XLA Ops:
  0.0 82.9 %copy-start.1 = (s32[192]{0:T(256)S(1)}, s32[192]{0:T(256)}, u32[]{:S(2)}) copy-start(s32[192]{0:T(256)} %constant.2.clone.table_ref) | copy-start | bytes 2308
  0.0 3.5 %copy-start = (bf16[128,4096]{1,0:T(8,128)(2,1)S(1)}, bf16[128,4096]{1,0:T(8,128)(2,1)}, u32[]{:S(2)}) copy-start(bf16[128,4096]{1,0:T(8,128)(2,1)} %own_ref.1) | copy-start | bytes 3145732
  0.0 82.9 %copy-start.3 = (s32[6]{0:T(128)S(1)}, s32[6]{0:T(128)}, u32[]{:S(2)}) copy-start(s32[6]{0:T(128)} %pad_ref.1) | copy-start | bytes 76
  0.0 82.9 %copy-start.2 = (s32[6]{0:T(128)S(1)}, s32[6]{0:T(128)}, u32[]{:S(2)}) copy-start(s32[6]{0:T(128)} %tiles_ref.1) | copy-start | bytes 76
  1.4 14.7 %collective-permute-start.4 = (bf16[64,4096]{1,0:T(8,128)(2,1)S(1)}, bf16[64,4096]{1,0:T(8,128)(2,1)S(1)}, u32[]{:S(2)}, u32[]{:S(2)}) collective-permute-start(bf16[64,4096]{1,0:T(8,128)(2,1)S(1)} %get-tuple-element.11), channel_id=1, source_target_pairs={{2,6},{3,7},{4,0},{5,1},{6,10},{7,11},{8,4},{9,5},{10,14},{11,15},... | collective-permute-start | bytes 1572872 | tf_op jit(solution)/shard_map/ppermute | solution.py:246
  3.5 39.3 %collective-permute-start.2 = (bf16[128,4096]{1,0:T(8,128)(2,1)S(1)}, bf16[128,4096]{1,0:T(8,128)(2,1)S(1)}, u32[]{:S(2)}, u32[]{:S(2)}) collective-permute-start(bf16[128,4096]{1,0:T(8,128)(2,1)S(1)} %copy-done), channel_id=1, source_target_pairs={{0,2},{1,3},{2,0},{3,1},{4,6},{5,7},{6,4},{7,5},{8,10},{9,11},{10,... | collective-permute-start | bytes 3145736 | tf_op jit(solution)/shard_map/ppermute | solution.py:246
  5.9 38.9 %collective-permute-start.3 = (bf16[128,4096]{1,0:T(8,128)(2,1)S(1)}, bf16[128,4096]{1,0:T(8,128)(2,1)S(1)}, u32[]{:S(2)}, u32[]{:S(2)}) collective-permute-start(bf16[128,4096]{1,0:T(8,128)(2,1)S(1)} %copy-done), channel_id=1, source_target_pairs={{0,4},{1,5},{4,8},{5,9},{6,2},{7,3},{8,12},{9,13},{10,6},{11,7},{1... | collective-permute-start | bytes 3145736 | tf_op jit(solution)/shard_map/ppermute | solution.py:246
  7.8 19.5 %collective-permute-start.1 = (bf16[64,4096]{1,0:T(8,128)(2,1)S(1)}, bf16[64,4096]{1,0:T(8,128)(2,1)S(1)}, u32[]{:S(2)}, u32[]{:S(2)}) collective-permute-start(bf16[64,4096]{1,0:T(8,128)(2,1)S(1)} %get-tuple-element.12), channel_id=1, source_target_pairs={{2,6},{3,7},{4,0},{5,1},{6,10},{7,11},{8,4},{9,5},{10,14},{11,15},... | collective-permute-start | bytes 1572872 | tf_op jit(solution)/shard_map/ppermute | solution.py:246
  16.1 12.8 %collective-permute-start.12 = (bf16[64,4096]{1,0:T(8,128)(2,1)S(1)}, bf16[64,4096]{1,0:T(8,128)(2,1)S(1)}, u32[]{:S(2)}, u32[]{:S(2)}) collective-permute-start(bf16[64,4096]{1,0:T(8,128)(2,1)S(1)} %collective-permute-done.4.rest_3_), channel_id=1, source_target_pairs={{4,0},{7,11},{8,4},{11,15},{20,16},{23,27},{24,20},{27,31}} | collective-permute-start | bytes 1572872 | tf_op jit(solution)/shard_map/ppermute | solution.py:246
  16.8 23.0 %collective-permute-start.6 = (bf16[64,4096]{1,0:T(8,128)(2,1)S(1)}, bf16[64,4096]{1,0:T(8,128)(2,1)S(1)}, u32[]{:S(2)}, u32[]{:S(2)}) collective-permute-start(bf16[64,4096]{1,0:T(8,128)(2,1)S(1)} %collective-permute-done.4.rest_3_), channel_id=1, source_target_pairs={{0,2},{1,3},{4,6},{5,7},{6,4},{7,5},{8,10},{9,11},{10,8},{11,9},{1... | collective-permute-start | bytes 1572872 | tf_op jit(solution)/shard_map/ppermute | solution.py:246
  27.3 28.1 %collective-permute-start = (bf16[128,4096]{1,0:T(8,128)(2,1)S(1)}, bf16[128,4096]{1,0:T(8,128)(2,1)S(1)}, u32[]{:S(2)}, u32[]{:S(2)}) collective-permute-start(bf16[128,4096]{1,0:T(8,128)(2,1)S(1)} %copy-done), channel_id=1, source_target_pairs={{0,1},{1,0},{2,3},{3,2},{4,5},{5,4},{6,7},{7,6},{8,9},{9,8},{10,11... | collective-permute-start | bytes 3145736 | tf_op jit(solution)/shard_map/ppermute | solution.py:247
  28.9 19.3 %collective-permute-start.11 = (bf16[64,4096]{1,0:T(8,128)(2,1)S(1)}, bf16[64,4096]{1,0:T(8,128)(2,1)S(1)}, u32[]{:S(2)}, u32[]{:S(2)}) collective-permute-start(bf16[64,4096]{1,0:T(8,128)(2,1)S(1)} %collective-permute-done.1.rest_0_), channel_id=1, source_target_pairs={{4,0},{7,11},{8,4},{11,15},{20,16},{23,27},{24,20},{27,31}} | collective-permute-start | bytes 1572872 | tf_op jit(solution)/shard_map/ppermute | solution.py:246
  39.7 13.8 %collective-permute-start.5 = (bf16[64,4096]{1,0:T(8,128)(2,1)S(1)}, bf16[64,4096]{1,0:T(8,128)(2,1)S(1)}, u32[]{:S(2)}, u32[]{:S(2)}) collective-permute-start(bf16[64,4096]{1,0:T(8,128)(2,1)S(1)} %collective-permute-done.1.rest_0_), channel_id=1, source_target_pairs={{0,2},{1,3},{4,6},{5,7},{6,4},{7,5},{8,10},{9,11},{10,8},{11,9},{1... | collective-permute-start | bytes 1572872 | tf_op jit(solution)/shard_map/ppermute | solution.py:246
  42.8 40.1 %collective-permute-start.8 = (bf16[128,4096]{1,0:T(8,128)(2,1)S(1)}, bf16[128,4096]{1,0:T(8,128)(2,1)S(1)}, u32[]{:S(2)}, u32[]{:S(2)}) collective-permute-start(bf16[128,4096]{1,0:T(8,128)(2,1)S(1)} %collective-permute-done.2.rest_1_), channel_id=1, source_target_pairs={{2,6},{3,7},{4,0},{5,1},{6,10},{7,11},{8,4},{9,5},{10,14},{11,15},... | collective-permute-start | bytes 3145736 | tf_op jit(solution)/shard_map/ppermute | solution.py:246
  44.9 38.0 %collective-permute-start.7 = (bf16[128,4096]{1,0:T(8,128)(2,1)S(1)}, bf16[128,4096]{1,0:T(8,128)(2,1)S(1)}, u32[]{:S(2)}, u32[]{:S(2)}) collective-permute-start(bf16[128,4096]{1,0:T(8,128)(2,1)S(1)} %collective-permute-done.3.rest_2_), channel_id=1, source_target_pairs={{5,9},{6,2},{9,13},{10,6},{21,25},{22,18},{25,29},{26,22}} | collective-permute-start | bytes 3145736 | tf_op jit(solution)/shard_map/ppermute | solution.py:246
  48.2 29.1 %collective-permute-start.10 = (bf16[64,4096]{1,0:T(8,128)(2,1)S(1)}, bf16[64,4096]{1,0:T(8,128)(2,1)S(1)}, u32[]{:S(2)}, u32[]{:S(2)}) collective-permute-start(bf16[64,4096]{1,0:T(8,128)(2,1)S(1)} %collective-permute-done.6.rest_5_), channel_id=1, source_target_pairs={{4,8},{5,9},{6,2},{7,3},{8,12},{9,13},{10,6},{11,7},{20,24},{21,25... | collective-permute-start | bytes 1572872 | tf_op jit(solution)/shard_map/ppermute | solution.py:246
  53.5 29.4 %collective-permute-start.9 = (bf16[64,4096]{1,0:T(8,128)(2,1)S(1)}, bf16[64,4096]{1,0:T(8,128)(2,1)S(1)}, u32[]{:S(2)}, u32[]{:S(2)}) collective-permute-start(bf16[64,4096]{1,0:T(8,128)(2,1)S(1)} %collective-permute-done.5.rest_4_), channel_id=1, source_target_pairs={{4,8},{5,9},{6,2},{7,3},{8,12},{9,13},{10,6},{11,7},{20,24},{21,25... | collective-permute-start | bytes 1572872 | tf_op jit(solution)/shard_map/ppermute | solution.py:246
  95.3 2.8 %collective-permute-start.13 = (bf16[128,4224]{1,0:T(8,128)(2,1)S(1)}, bf16[128,4224]{1,0:T(8,128)(2,1)S(1)}, u32[]{:S(2)}, u32[]{:S(2)}) collective-permute-start(bf16[128,4224]{1,0:T(8,128)(2,1)S(1)} %get-tuple-element.8), channel_id=1, source_target_pairs={{0,1},{1,0},{2,3},{3,2},{4,5},{5,4},{6,7},{7,6},{8,9},{9,8},{10,11... | collective-permute-start | bytes 3244040 | tf_op jit(solution)/shard_map/ppermute | solution.py:250

commit v2 on v1

v2 whole, which is shorter than its diff:
```python
import functools

import jax
import jax.numpy as jnp
from jax import lax
from jax.experimental import pallas as pl
from jax.experimental.pallas import tpu as pltpu
from jax.sharding import PartitionSpec as P

MOST = 8
TILE = 128
HALF = 64

similarity_scale = 64.0


def across(row, column, core):
    return row, 1 - column


def along(row, column, core):
    return row + 2 * column - 1, column


def against(row, column, core):
    return row + 1 - 2 * column, column


def straight(row, column, core):
    return row + 2 * core - 1, column


STEPS = (
    ("a", "e", along),
    ("b", "e", against),
    ("y", "e", across),
    ("w0", ("a", 0), across),
    ("x", "y", along),
    ("w1", ("a", 1), across),
    ("r0", "w0", against),
    ("s", "ab", straight),
    ("r1", "w1", against),
)


def routes(tiles):
    held, sizes = {"e": [2 * d for d in range(tiles)]}, {"e": TILE}
    pairs, rows, table = [], [], []
    for name, value, direction in STEPS:
        if isinstance(value, tuple):
            carried, size = [piece + value[1] if piece >= 0 else -1 for piece in held[value[0]]], HALF
        else:
            carried, size = held[value], sizes[value]
        landed, moves = [-1] * tiles, []
        for source in range(tiles):
            target = direction(source // 4, source // 2 % 2, source % 2)
            if not 0 <= target[0] < tiles // 4 or carried[source] < 0:
                continue
            place = 4 * target[0] + 2 * target[1] + source % 2
            moves.append((source, place))
            landed[place] = carried[source]
        held[name], sizes[name] = landed, size
        if name == "b":
            held["ab"] = [held["a" if d % 2 == d // 2 % 2 else "b"][d] for d in range(tiles)]
            sizes["ab"] = TILE
        pairs.append(tuple(moves))
        rows.append(size)
        table.append(landed)
    for device in range(tiles):
        got = []
        for landed, count in zip(table, rows):
            if landed[device] >= 0:
                got += [landed[device]] if count == HALF else [landed[device], landed[device] + 1]
        assert len(got) == len(set(got))
        for tile in (device, device ^ 1):
            for far in range(max(0, tile - MOST + 1), min(tiles, tile + MOST)):
                if far % 2 == device % 2 and far != device:
                    assert {2 * far, 2 * far + 1} <= set(got), (device, far)
    return pairs, rows, table


def attend_kernel(rows, bounds, clusters, early, tiles_ref, pad_ref, table_ref, *rest):
    own_ref, sib_ref = rest[:2]
    pieces = rest[2 : 2 + len(rows)]
    rest = rest[2 + len(rows) :]
    if not early:
        own_in, sib_in = rest[:2]
        rest = rest[2:]
    own_out, sib_out, held, weights, limits, den, sems = rest
    width = own_ref.shape[1]
    me = lax.axis_index("tiles")
    other = me + 1 - 2 * lax.rem(me, 2)
    base = TILE if early else 2 * TILE

    def layout(tile):
        start, cluster, live = jnp.int32(0), jnp.int32(-1), jnp.int32(0)
        for c in range(clusters):
            count = tiles_ref[c]
            inside = (start <= tile) & (tile < start + count)
            cluster = jnp.where(inside, c, cluster)
            live = jnp.where(inside, count * TILE - pad_ref[c] - (tile - start) * TILE, live)
            start = start + count
        return cluster, jnp.clip(live, 0, TILE)

    copies = [
        pltpu.make_async_copy(sib_ref, held.at[pl.ds(0, TILE)], sems.at[0]),
        pltpu.make_async_copy(own_ref, held.at[pl.ds(TILE, TILE)], sems.at[1]),
    ]
    for copy in copies:
        copy.start()
    own_cluster, own_live = layout(me)
    sib_cluster, sib_live = layout(other)

    def note(unit, cluster, live):
        limits[0, unit] = jnp.where(cluster == own_cluster, jnp.clip(live, 0, HALF), 0)
        limits[1, unit] = jnp.where(cluster == sib_cluster, jnp.clip(live, 0, HALF), 0)

    if early:
        note(0, own_cluster, own_live)
        note(1, own_cluster, own_live - HALF)

    used = jnp.int32(2 if early else 0)
    pending = []
    for i, count in enumerate(rows):
        piece = table_ref[me * len(rows) + i]
        cluster, live = layout(lax.shift_right_arithmetic(piece, 1))
        live = live - HALF * (piece & 1)
        valid = (piece >= 0) & ((cluster == own_cluster) | (cluster == sib_cluster))
        place = pl.multiple_of(base + used * HALF, HALF)
        copy = pltpu.make_async_copy(pieces[i], held.at[pl.ds(place, count)], sems.at[2 + i])

        @pl.when(valid)
        def _(copy=copy, used=used, cluster=cluster, live=live, count=count):
            copy.start()
            note(used, cluster, live)
            if count == TILE:
                note(used + 1, cluster, live - HALF)

        pending.append((valid, copy))
        used = used + jnp.where(valid, count // HALF, 0)

    bound = jnp.int32(bounds[-1])
    for smaller in reversed(bounds[:-1]):
        bound = jnp.where(used <= smaller, smaller, bound)
    for unit in range(2 if early else 0, bounds[-1]):

        @pl.when((unit >= used) & (unit < bound))
        def _(unit=unit):
            held[pl.ds(base + unit * HALF, HALF), :] = jnp.zeros((HALF, width), held.dtype)
            limits[0, unit] = jnp.int32(0)
            limits[1, unit] = jnp.int32(0)

    for copy in copies:
        copy.wait()
    for valid, copy in pending:

        @pl.when(valid)
        def _(copy=copy):
            copy.wait()

    def inverse(at):
        wide = held[at, :].astype(jnp.float32)
        return lax.rsqrt(jnp.sum(wide * wide, axis=1, keepdims=True) + 1e-06)

    wide = 2 * TILE
    if early:
        inv_rows = jnp.concatenate([inverse(pl.ds(0, TILE)), inverse(pl.ds(TILE, TILE))], axis=0)
        sib_out[:, pl.ds(width + TILE, TILE)] = jnp.broadcast_to(inv_rows[:TILE], (TILE, TILE))
        own_out[:, pl.ds(width + TILE, TILE)] = jnp.broadcast_to(inv_rows[TILE:], (TILE, TILE))
        den[...] = jnp.zeros_like(den)
    else:
        at = pl.ds(width + TILE, TILE)
        inv_rows = jnp.concatenate([sib_in[:, at], own_in[:, at]], axis=0)[:, 0:1]
        at = pl.ds(width, TILE)
        den[pl.ds(0, TILE), :] = sib_in[:, at]
        den[pl.ds(TILE, TILE), :] = own_in[:, at]
    row = lax.broadcasted_iota(jnp.int32, (wide, wide), 0)
    lane = lax.broadcasted_iota(jnp.int32, (wide, wide), 1)
    is_sib = row < TILE
    row_live = row < jnp.where(is_sib, sib_live, own_live + TILE)

    @pl.loop(0, bound // 4)
    def _(b):
        start = pl.multiple_of(base + b * wide, TILE)
        gram = lax.dot_general(
            held[pl.ds(0, wide), :],
            held[pl.ds(start, wide), :],
            (((1,), (1,)), ((), ())),
            preferred_element_type=jnp.float32,
        )
        inv_columns = jnp.concatenate(
            [
                jnp.broadcast_to(inverse(pl.ds(pl.multiple_of(start + at, TILE), TILE)), (TILE, TILE)).T[0:1, :]
                for at in (0, TILE)
            ],
            axis=1,
        )
        scores = similarity_scale * inv_rows * inv_columns * gram
        end = jnp.int32(0)
        for u in reversed(range(4)):
            here = u * HALF + jnp.where(is_sib, limits[1, 4 * b + u], limits[0, 4 * b + u])
            end = here if u == 3 else jnp.where(lane < (u + 1) * HALF, here, end)
        keep = row_live & (lane < end)
        if early:
            keep = keep & ((row - TILE != lane) | (b != 0))
        block = jnp.where(keep, jnp.exp(scores), 0.0).astype(jnp.bfloat16)
        weights[:, pl.ds(pl.multiple_of(b * wide, wide), wide)] = block
        den[...] += jnp.broadcast_to(jnp.sum(block.astype(jnp.float32), axis=1, keepdims=True), den.shape)

    chunk = 512

    def products(depth):
        @pl.loop(0, width // chunk)
        def _(f):
            at = pl.ds(pl.multiple_of(f * chunk, chunk), chunk)
            total = jnp.dot(
                weights[:, pl.ds(0, depth)], held[pl.ds(base, depth), at], preferred_element_type=jnp.float32
            )
            if early:
                sib_out[:, at] = total[:TILE]
                own_out[:, at] = total[TILE:]
            else:
                sib_out[:, at] = (sib_in[:, at] + total[:TILE]).astype(jnp.bfloat16)
                own_out[:, at] = own_in[:, at] + total[TILE:]

    for depth in bounds:

        @pl.when(bound == depth)
        def _(depth=depth):
            products(depth * HALF)

    own_out[:, pl.ds(width, TILE)] = den[pl.ds(TILE, TILE), :]
    whole = den[pl.ds(0, TILE), :]
    if early:
        sib_out[:, pl.ds(width, TILE)] = whole
        return
    first = whole.astype(jnp.bfloat16).astype(jnp.float32)
    second = (whole - first).astype(jnp.bfloat16).astype(jnp.float32)
    third = whole - first - second
    part = lax.broadcasted_iota(jnp.int32, (TILE, TILE), 1)
    sib_out[:, pl.ds(width, TILE)] = jnp.where(
        part == 0, first, jnp.where(part == 1, second, jnp.where(part == 2, third, 0.0))
    ).astype(jnp.bfloat16)


def attend(tiles, routed, names, cluster_tiles, last_tile_pad, own, sibling, held, sums=None):
    early = sums is None
    chosen = [i for i, step in enumerate(STEPS) if step[0] in names]
    rows = tuple(routed[1][i] for i in chosen)
    width = own.shape[1]
    flat = jnp.array([routed[2][i][d] for d in range(tiles) for i in chosen], jnp.int32)
    bounds = (4, 8)
    base = TILE if early else 2 * TILE
    assert bounds[-1] * HALF >= sum(rows) + TILE * early
    smem = pl.BlockSpec(memory_space=pltpu.SMEM)
    anywhere = pl.BlockSpec(memory_space=pl.ANY)
    vmem = pl.BlockSpec(memory_space=pltpu.VMEM)
    if early:
        outs = (jax.ShapeDtypeStruct((TILE, width + 2 * TILE), jnp.float32),) * 2
    else:
        outs = tuple(jax.ShapeDtypeStruct((TILE, width + TILE), kind) for kind in (jnp.float32, jnp.bfloat16))
    columns = sum(rows) + TILE * early
    return pl.pallas_call(
        functools.partial(attend_kernel, rows, bounds, cluster_tiles.shape[0], early),
        out_shape=outs,
        in_specs=[smem] * 3 + [anywhere] * (2 + len(rows)) + [vmem] * (0 if early else 2),
        out_specs=(vmem, vmem),
        scratch_shapes=[
            pltpu.VMEM((base + bounds[-1] * HALF, width), jnp.bfloat16),
            pltpu.VMEM((2 * TILE, bounds[-1] * HALF), jnp.bfloat16),
            pltpu.SMEM((2, bounds[-1]), jnp.int32),
            pltpu.VMEM((2 * TILE, TILE), jnp.float32),
            pltpu.SemaphoreType.DMA((2 + len(rows),)),
        ],
        compiler_params=pltpu.CompilerParams(vmem_limit_bytes=32 * 1024 * 1024),
        cost_estimate=pl.CostEstimate(
            flops=8 * TILE * columns * width, bytes_accessed=2 * (columns + 2 * TILE) * width, transcendentals=0
        ),
    )(cluster_tiles, last_tile_pad, flat, own, sibling, *[held[STEPS[i][0]] for i in chosen], *(sums or ()))


FIRST = ("a", "b", "y")


def body(embeddings, cluster_tiles, last_tile_pad):
    width = embeddings.shape[1]
    tiles = lax.axis_size("tiles")
    routed = routes(tiles)
    cores = [(i, i ^ 1) for i in range(tiles)]
    pairs = {step[0]: moves for step, moves in zip(STEPS, routed[0])}
    values = {step[0]: step[1] for step in STEPS}
    held = {"e": embeddings}

    def send(name):
        value = values[name]
        if isinstance(value, tuple):
            operand = held[value[0]][value[1] * HALF : (value[1] + 1) * HALF]
        else:
            operand = held[value]
        held[name] = lax.ppermute(operand, "tiles", pairs[name])

    def together(*names):
        held.update(zip(names, lax.optimization_barrier(tuple(held[name] for name in names))))

    for name in FIRST:
        send(name)
    held["sib"] = lax.ppermute(embeddings, "tiles", cores)
    together("sib", "b", "y", "a")
    send("w0")
    send("x")
    me = lax.axis_index("tiles")
    held["ab"] = jnp.where(me % 2 == me // 2 % 2, held["a"], held["b"])
    send("s")
    together("a", "w0")
    for name in ("r0", "w1", "r1"):
        send(name)
    sibling = held["sib"]
    common = (cluster_tiles, last_tile_pad, embeddings, sibling, held)
    sums = attend(tiles, routed, FIRST, *common)
    rest = [step[0] for step in STEPS if step[0] not in FIRST]
    own_sum, sib_sum = attend(tiles, routed, rest, *common, sums)
    other_sum = lax.ppermute(sib_sum, "tiles", cores)
    numer = own_sum[:, :width] + other_sum[:, :width].astype(jnp.float32)
    parts = other_sum[:, width : width + 3].astype(jnp.float32)
    denom = own_sum[:, width] + (parts[:, 0] + parts[:, 1] + parts[:, 2])
    live = denom > 0.0
    return jnp.where(live[:, None], numer / jnp.where(live, denom, 1.0)[:, None], 0.0).astype(jnp.bfloat16)


def solution(mesh):
    placed = (P(("groups", "tiles"), None), P("groups"), P("groups"))
    return jax.shard_map(
        body, mesh=mesh, in_specs=placed, out_specs=P(("groups", "tiles"), None), check_vma=False
    )
```

time: 100 us -> 84.4 us (0.84)
  the two profiles are of different devices: /device:TPU:17 before, /device:TPU:0 now
where the time goes in v2:
time: 84.4 us; the launch traced here: 83.4 us
  waiting for transfers between devices  49.6 us (59%)
  starting transfers between devices  21.8 us (26%)
  Pallas kernels  9.92 us (12%)
  other arithmetic  1.79 us (2%)
    ppermute x9, waiting for transfers between devices, send(): held[name] = lax.ppermute(operand, 'tiles', pairs[name])  46.9 us
    ppermute x9, starting transfers between devices, send(): held[name] = lax.ppermute(operand, 'tiles', pairs[name])  21.7 us
    pallas_call x2, Pallas kernels, attend(): pl.pallas_call(functools.partial(attend_kernel, rows, bounds, cluster_til...  9.92 us
    ppermute x1, waiting for transfers between devices, body(): other_sum = lax.ppermute(sib_sum, 'tiles', cores)  2.69 us
  transfers between devices with their start and end apart: 11, of which 7 were waited for; matrix products, arithmetic and copies ran while one was open for 0% of the time, Pallas kernels for 7%

profile of v2, /device:TPU:0, one launch (start us, length us, event | category | flops | bytes accessed | tf_op | source)
XLA Modules:
  0.0 83.4 jit_solution(18288023434120118231)
XLA Ops:
  0.0 1.3 %collective-permute-start.3 = (bf16[128,4096]{1,0:T(8,128)(2,1)}, bf16[128,4096]{1,0:T(8,128)(2,1)S(1)}, u32[]{:S(2)}, u32[]{:S(2)}) collective-permute-start(bf16[128,4096]{1,0:T(8,128)(2,1)} %rest_0_.3), channel_id=1, source_target_pairs={{2,6},{3,7},{4,0},{5,1},{6,10},{7,11},{8,4},{9,5},{10,14},{11,15},... | collective-permute-start | bytes 3145736 | tf_op jit(solution)/shard_map/ppermute | solution.py:300
  1.3 5.3 %collective-permute-start.2 = (bf16[128,4096]{1,0:T(8,128)(2,1)}, bf16[128,4096]{1,0:T(8,128)(2,1)}, u32[]{:S(2)}, u32[]{:S(2)}) collective-permute-start(bf16[128,4096]{1,0:T(8,128)(2,1)} %rest_0_.3), channel_id=1, source_target_pairs={{0,2},{1,3},{2,0},{3,1},{4,6},{5,7},{6,4},{7,5},{8,10},{9,11},{10,... | collective-permute-start | bytes 3145736 | tf_op jit(solution)/shard_map/ppermute | solution.py:300
  6.6 3.5 %collective-permute-start.1 = (bf16[128,4096]{1,0:T(8,128)(2,1)}, bf16[128,4096]{1,0:T(8,128)(2,1)S(1)}, u32[]{:S(2)}, u32[]{:S(2)}) collective-permute-start(bf16[128,4096]{1,0:T(8,128)(2,1)} %rest_0_.3), channel_id=1, source_target_pairs={{0,4},{1,5},{4,8},{5,9},{6,2},{7,3},{8,12},{9,13},{10,6},{11,7},{1... | collective-permute-start | bytes 3145736 | tf_op jit(solution)/shard_map/ppermute | solution.py:300
  10.1 0.1 collective-permute-start
  10.2 18.1 %collective-permute-done.3.rest_2_ = bf16[128,4096]{1,0:T(8,128)(2,1)S(1)} collective-permute-done((bf16[128,4096]{1,0:T(8,128)(2,1)}, bf16[128,4096]{1,0:T(8,128)(2,1)S(1)}, u32[]{:S(2)}, u32[]{:S(2)}) %collective-permute-start.3) | collective-permute-done | bytes 1048608 | tf_op jit(solution)/shard_map/ppermute | solution.py:300
  28.3 1.5 %collective-permute-done.2.rest_4_ = bf16[128,4096]{1,0:T(8,128)(2,1)} collective-permute-done((bf16[128,4096]{1,0:T(8,128)(2,1)}, bf16[128,4096]{1,0:T(8,128)(2,1)}, u32[]{:S(2)}, u32[]{:S(2)}) %collective-permute-start.2) | collective-permute-done | bytes 1048608 | tf_op jit(solution)/shard_map/ppermute | solution.py:300
  29.8 2.4 %collective-permute-done.1.rest_3_ = bf16[128,4096]{1,0:T(8,128)(2,1)S(1)} collective-permute-done((bf16[128,4096]{1,0:T(8,128)(2,1)}, bf16[128,4096]{1,0:T(8,128)(2,1)S(1)}, u32[]{:S(2)}, u32[]{:S(2)}) %collective-permute-start.1) | collective-permute-done | bytes 1048608 | tf_op jit(solution)/shard_map/ppermute | solution.py:300
  32.1 0.0 collective-permute-done.rest_1_
  32.2 0.0 copy-start
  32.2 0.0 copy-start.1
  32.2 0.0 copy-start.2
  32.2 0.0 copy-start.4
  32.2 3.2 %collective-permute-start.4 = (bf16[64,4096]{1,0:T(8,128)(2,1)S(1)}, bf16[64,4096]{1,0:T(8,128)(2,1)S(1)}, u32[]{:S(2)}, u32[]{:S(2)}) collective-permute-start(bf16[64,4096]{1,0:T(8,128)(2,1)S(1)} %slice.27), channel_id=1, source_target_pairs={{0,2},{1,3},{4,6},{5,7},{6,4},{7,5},{8,10},{9,11},{10,8},{11,9},{1... | collective-permute-start | bytes 1572872 | tf_op jit(solution)/shard_map/ppermute | solution.py:300
  35.5 0.1 broadcast_select_fusion
  35.6 1.3 %collective-permute-start.8 = (bf16[128,4096]{1,0:T(8,128)(2,1)S(1)}, bf16[128,4096]{1,0:T(8,128)(2,1)S(1)}, u32[]{:S(2)}, u32[]{:S(2)}) collective-permute-start(bf16[128,4096]{1,0:T(8,128)(2,1)S(1)} %broadcast_select_fusion), channel_id=1, source_target_pairs={{4,0},{5,9},{6,2},{7,11},{8,4},{9,13},{10,6},{11,15},{20,16},{21,2... | collective-permute-start | bytes 3145736 | tf_op jit(solution)/shard_map/ppermute | solution.py:300
  36.9 1.3 %collective-permute-start.5 = (bf16[128,4096]{1,0:T(8,128)(2,1)}, bf16[128,4096]{1,0:T(8,128)(2,1)S(1)}, u32[]{:S(2)}, u32[]{:S(2)}) collective-permute-start(bf16[128,4096]{1,0:T(8,128)(2,1)} %collective-permute-done.2.rest_4_), channel_id=1, source_target_pairs={{2,6},{3,7},{4,0},{5,1},{6,10},{7,11},{8,4},{9,5},{10,14},{11,15},... | collective-permute-start | bytes 3145736 | tf_op jit(solution)/shard_map/ppermute | solution.py:300
  38.2 7.2 %collective-permute-done.4.rest_2_ = bf16[64,4096]{1,0:T(8,128)(2,1)S(1)} collective-permute-done((bf16[64,4096]{1,0:T(8,128)(2,1)S(1)}, bf16[64,4096]{1,0:T(8,128)(2,1)S(1)}, u32[]{:S(2)}, u32[]{:S(2)}) %collective-permute-start.4) | collective-permute-done | bytes 524320 | tf_op jit(solution)/shard_map/ppermute | solution.py:300
  45.5 0.0 copy-start.3
  45.5 4.4 %collective-permute-start.6 = (bf16[64,4096]{1,0:T(8,128)(2,1)S(1)}, bf16[64,4096]{1,0:T(8,128)(2,1)S(1)}, u32[]{:S(2)}, u32[]{:S(2)}) collective-permute-start(bf16[64,4096]{1,0:T(8,128)(2,1)S(1)} %slice.28), channel_id=1, source_target_pairs={{0,2},{1,3},{4,6},{5,7},{6,4},{7,5},{8,10},{9,11},{10,8},{11,9},{1... | collective-permute-start | bytes 1572872 | tf_op jit(solution)/shard_map/ppermute | solution.py:300
  49.9 0.7 collective-permute-start.7
  50.6 8.3 %collective-permute-done.6.rest_4_ = bf16[64,4096]{1,0:T(8,128)(2,1)S(1)} collective-permute-done((bf16[64,4096]{1,0:T(8,128)(2,1)S(1)}, bf16[64,4096]{1,0:T(8,128)(2,1)S(1)}, u32[]{:S(2)}, u32[]{:S(2)}) %collective-permute-start.6) | collective-permute-done | bytes 524320 | tf_op jit(solution)/shard_map/ppermute | solution.py:300
  58.9 0.7 collective-permute-start.9
  59.7 5.7 %shard_map.55 = (f32[128,4352]{1,0:T(8,128)S(1)}, f32[128,4352]{1,0:T(8,128)S(1)}) custom-call(s32[6]{0:T(128)S(1)} %copy-done.1, s32[6]{0:T(128)S(1)} %copy-done.2, s32[48]{0:T(128)S(1)} %copy-done.4, bf16[128,4096]{1,0:T(8,128)(2,1)S(1)} %copy-done, bf16[128,4096]{1,0:T(8,128)(2,1)S(1)} %collective-permute-done.rest_1_, ...), custom_call_target="tpu_custom_call" | custom-call | flops 2147483648 | bytes 6291456 | tf_op jit(solution)/shard_map/pallas_call | solution.py:263
  65.4 0.0 collective-permute-done.7.rest_5_
  65.4 9.4 %collective-permute-done.5.rest_3_ = bf16[128,4096]{1,0:T(8,128)(2,1)S(1)} collective-permute-done((bf16[128,4096]{1,0:T(8,128)(2,1)}, bf16[128,4096]{1,0:T(8,128)(2,1)S(1)}, u32[]{:S(2)}, u32[]{:S(2)}) %collective-permute-start.5) | collective-permute-done | bytes 1048608 | tf_op jit(solution)/shard_map/ppermute | solution.py:300
  74.8 0.0 collective-permute-done.9.rest_7_
  74.8 4.2 %shard_map.56 = (f32[128,4224]{1,0:T(8,128)S(1)}, bf16[128,4224]{1,0:T(8,128)(2,1)S(1)}) custom-call(s32[6]{0:T(128)S(1)} %copy-done.1, s32[6]{0:T(128)S(1)} %copy-done.2, s32[96]{0:T(128)S(1)} %copy-done.3, bf16[128,4096]{1,0:T(8,128)(2,1)S(1)} %copy-done, bf16[128,4096]{1,0:T(8,128)(2,1)S(1)} %collective-permute-done.rest_1_, ...), custom_call_target="tpu_custom_call" | custom-call | flops 2147483648 | bytes 6291456 | tf_op jit(solution)/shard_map/pallas_call | solution.py:263
  79.0 0.1 collective-permute-start.10
  79.1 2.7 %collective-permute-done.10 = bf16[128,4224]{1,0:T(8,128)(2,1)S(1)} collective-permute-done((bf16[128,4224]{1,0:T(8,128)(2,1)S(1)}, bf16[128,4224]{1,0:T(8,128)(2,1)S(1)}, u32[]{:S(2)}, u32[]{:S(2)}) %collective-permute-start.10) | collective-permute-done | bytes 1081376 | tf_op jit(solution)/shard_map/ppermute | solution.py:322
  81.8 0.2 compare_reduce_fusion
  81.9 0.1 fusion
  82.1 1.4 %select_convert_fusion = bf16[128,4096]{1,0:T(8,128)(2,1)} fusion(f32[128,4224]{1,0:T(8,128)S(1)} %get-tuple-element.23, bf16[128,4224]{1,0:T(8,128)(2,1)S(1)} %collective-permute-done.10, f32[128]{0:T(128)S(1)} %fusion, pred[128]{0:T(512)(128)(4,1)S(1)} %get-tuple-element.25), kind=kLoop, calls=%fused_computation | loop fusion | flops 2621440 | bytes 4194944 | tf_op jit(solution)/shard_map/convert_element_type | solution.py:327
  (9 shorter events, 0.1 us)
Async XLA Ops:
  0.0 28.3 %collective-permute-start.3 = (bf16[128,4096]{1,0:T(8,128)(2,1)}, bf16[128,4096]{1,0:T(8,128)(2,1)S(1)}, u32[]{:S(2)}, u32[]{:S(2)}) collective-permute-start(bf16[128,4096]{1,0:T(8,128)(2,1)} %rest_0_.3), channel_id=1, source_target_pairs={{2,6},{3,7},{4,0},{5,1},{6,10},{7,11},{8,4},{9,5},{10,14},{11,15},... | collective-permute-start | bytes 3145736 | tf_op jit(solution)/shard_map/ppermute | solution.py:300
  1.3 28.5 %collective-permute-start.2 = (bf16[128,4096]{1,0:T(8,128)(2,1)}, bf16[128,4096]{1,0:T(8,128)(2,1)}, u32[]{:S(2)}, u32[]{:S(2)}) collective-permute-start(bf16[128,4096]{1,0:T(8,128)(2,1)} %rest_0_.3), channel_id=1, source_target_pairs={{0,2},{1,3},{2,0},{3,1},{4,6},{5,7},{6,4},{7,5},{8,10},{9,11},{10,... | collective-permute-start | bytes 3145736 | tf_op jit(solution)/shard_map/ppermute | solution.py:300
  6.6 25.6 %collective-permute-start.1 = (bf16[128,4096]{1,0:T(8,128)(2,1)}, bf16[128,4096]{1,0:T(8,128)(2,1)S(1)}, u32[]{:S(2)}, u32[]{:S(2)}) collective-permute-start(bf16[128,4096]{1,0:T(8,128)(2,1)} %rest_0_.3), channel_id=1, source_target_pairs={{0,4},{1,5},{4,8},{5,9},{6,2},{7,3},{8,12},{9,13},{10,6},{11,7},{1... | collective-permute-start | bytes 3145736 | tf_op jit(solution)/shard_map/ppermute | solution.py:300
  10.1 22.1 %collective-permute-start = (bf16[128,4096]{1,0:T(8,128)(2,1)}, bf16[128,4096]{1,0:T(8,128)(2,1)S(1)}, u32[]{:S(2)}, u32[]{:S(2)}) collective-permute-start(bf16[128,4096]{1,0:T(8,128)(2,1)} %rest_0_.3), channel_id=1, source_target_pairs={{0,1},{1,0},{2,3},{3,2},{4,5},{5,4},{6,7},{7,6},{8,9},{9,8},{10,11... | collective-permute-start | bytes 3145736 | tf_op jit(solution)/shard_map/ppermute | solution.py:307
  32.2 27.4 %copy-start = (bf16[128,4096]{1,0:T(8,128)(2,1)S(1)}, bf16[128,4096]{1,0:T(8,128)(2,1)}, u32[]{:S(2)}) copy-start(bf16[128,4096]{1,0:T(8,128)(2,1)} %rest_0_.3) | copy-start | bytes 3145732
  32.2 27.4 %copy-start.1 = (s32[6]{0:T(128)S(1)}, s32[6]{0:T(128)}, u32[]{:S(2)}) copy-start(s32[6]{0:T(128)} %tiles_ref.3) | copy-start | bytes 76
  32.2 27.4 %copy-start.2 = (s32[6]{0:T(128)S(1)}, s32[6]{0:T(128)}, u32[]{:S(2)}) copy-start(s32[6]{0:T(128)} %pad_ref.3) | copy-start | bytes 76
  32.2 27.4 %copy-start.4 = (s32[48]{0:T(128)S(1)}, s32[48]{0:T(128)}, u32[]{:S(2)}) copy-start(s32[48]{0:T(128)} %constant.41.clone.table_ref) | copy-start | bytes 580
  32.2 13.2 %collective-permute-start.4 = (bf16[64,4096]{1,0:T(8,128)(2,1)S(1)}, bf16[64,4096]{1,0:T(8,128)(2,1)S(1)}, u32[]{:S(2)}, u32[]{:S(2)}) collective-permute-start(bf16[64,4096]{1,0:T(8,128)(2,1)S(1)} %slice.27), channel_id=1, source_target_pairs={{0,2},{1,3},{4,6},{5,7},{6,4},{7,5},{8,10},{9,11},{10,8},{11,9},{1... | collective-permute-start | bytes 1572872 | tf_op jit(solution)/shard_map/ppermute | solution.py:300
  35.6 29.8 %collective-permute-start.8 = (bf16[128,4096]{1,0:T(8,128)(2,1)S(1)}, bf16[128,4096]{1,0:T(8,128)(2,1)S(1)}, u32[]{:S(2)}, u32[]{:S(2)}) collective-permute-start(bf16[128,4096]{1,0:T(8,128)(2,1)S(1)} %broadcast_select_fusion), channel_id=1, source_target_pairs={{4,0},{5,9},{6,2},{7,11},{8,4},{9,13},{10,6},{11,15},{20,16},{21,2... | collective-permute-start | bytes 3145736 | tf_op jit(solution)/shard_map/ppermute | solution.py:300
  36.9 37.9 %collective-permute-start.5 = (bf16[128,4096]{1,0:T(8,128)(2,1)}, bf16[128,4096]{1,0:T(8,128)(2,1)S(1)}, u32[]{:S(2)}, u32[]{:S(2)}) collective-permute-start(bf16[128,4096]{1,0:T(8,128)(2,1)} %collective-permute-done.2.rest_4_), channel_id=1, source_target_pairs={{2,6},{3,7},{4,0},{5,1},{6,10},{7,11},{8,4},{9,5},{10,14},{11,15},... | collective-permute-start | bytes 3145736 | tf_op jit(solution)/shard_map/ppermute | solution.py:300
  45.5 29.3 %copy-start.3 = (s32[96]{0:T(128)S(1)}, s32[96]{0:T(128)}, u32[]{:S(2)}) copy-start(s32[96]{0:T(128)} %constant.42.clone.table_ref) | copy-start | bytes 1156
  45.5 13.4 %collective-permute-start.6 = (bf16[64,4096]{1,0:T(8,128)(2,1)S(1)}, bf16[64,4096]{1,0:T(8,128)(2,1)S(1)}, u32[]{:S(2)}, u32[]{:S(2)}) collective-permute-start(bf16[64,4096]{1,0:T(8,128)(2,1)S(1)} %slice.28), channel_id=1, source_target_pairs={{0,2},{1,3},{4,6},{5,7},{6,4},{7,5},{8,10},{9,11},{10,8},{11,9},{1... | collective-permute-start | bytes 1572872 | tf_op jit(solution)/shard_map/ppermute | solution.py:300
  49.9 15.5 %collective-permute-start.7 = (bf16[64,4096]{1,0:T(8,128)(2,1)S(1)}, bf16[64,4096]{1,0:T(8,128)(2,1)S(1)}, u32[]{:S(2)}, u32[]{:S(2)}) collective-permute-start(bf16[64,4096]{1,0:T(8,128)(2,1)S(1)} %collective-permute-done.4.rest_2_), channel_id=1, source_target_pairs={{4,8},{5,9},{6,2},{7,3},{8,12},{9,13},{10,6},{11,7},{20,24},{21,25... | collective-permute-start | bytes 1572872 | tf_op jit(solution)/shard_map/ppermute | solution.py:300
  58.9 15.8 %collective-permute-start.9 = (bf16[64,4096]{1,0:T(8,128)(2,1)S(1)}, bf16[64,4096]{1,0:T(8,128)(2,1)S(1)}, u32[]{:S(2)}, u32[]{:S(2)}) collective-permute-start(bf16[64,4096]{1,0:T(8,128)(2,1)S(1)} %collective-permute-done.6.rest_4_), channel_id=1, source_target_pairs={{4,8},{5,9},{6,2},{7,3},{8,12},{9,13},{10,6},{11,7},{20,24},{21,25... | collective-permute-start | bytes 1572872 | tf_op jit(solution)/shard_map/ppermute | solution.py:300
  79.0 2.8 %collective-permute-start.10 = (bf16[128,4224]{1,0:T(8,128)(2,1)S(1)}, bf16[128,4224]{1,0:T(8,128)(2,1)S(1)}, u32[]{:S(2)}, u32[]{:S(2)}) collective-permute-start(bf16[128,4224]{1,0:T(8,128)(2,1)S(1)} %get-tuple-element.24), channel_id=1, source_target_pairs={{0,1},{1,0},{2,3},{3,2},{4,5},{5,4},{6,7},{7,6},{8,9},{9,8},{10,11... | collective-permute-start | bytes 3244040 | tf_op jit(solution)/shard_map/ppermute | solution.py:322

commit v3 on v2

--- a/solution.py
+++ b/solution.py
@@ -79,7 +79,7 @@
     return pairs, rows, table
 
 
-def attend_kernel(rows, bounds, clusters, early, tiles_ref, pad_ref, table_ref, *rest):
+def attend_kernel(rows, bounds, clusters, early, late, tiles_ref, pad_ref, table_ref, *rest):
     own_ref, sib_ref = rest[:2]
     pieces = rest[2 : 2 + len(rows)]
     rest = rest[2 + len(rows) :]
@@ -171,6 +171,9 @@
     else:
         at = pl.ds(width + TILE, TILE)
         inv_rows = jnp.concatenate([sib_in[:, at], own_in[:, at]], axis=0)[:, 0:1]
+        if not late:
+            sib_out[:, at] = sib_in[:, at]
+            own_out[:, at] = own_in[:, at]
         at = pl.ds(width, TILE)
         den[pl.ds(0, TILE), :] = sib_in[:, at]
         den[pl.ds(TILE, TILE), :] = own_in[:, at]
@@ -220,7 +223,7 @@
                 sib_out[:, at] = total[:TILE]
                 own_out[:, at] = total[TILE:]
             else:
-                sib_out[:, at] = (sib_in[:, at] + total[:TILE]).astype(jnp.bfloat16)
+                sib_out[:, at] = (sib_in[:, at] + total[:TILE]).astype(sib_out.dtype)
                 own_out[:, at] = own_in[:, at] + total[TILE:]
 
     for depth in bounds:
@@ -231,7 +234,7 @@
 
     own_out[:, pl.ds(width, TILE)] = den[pl.ds(TILE, TILE), :]
     whole = den[pl.ds(0, TILE), :]
-    if early:
+    if not late:
         sib_out[:, pl.ds(width, TILE)] = whole
         return
     first = whole.astype(jnp.bfloat16).astype(jnp.float32)
@@ -243,25 +246,25 @@
     ).astype(jnp.bfloat16)
 
 
-def attend(tiles, routed, names, cluster_tiles, last_tile_pad, own, sibling, held, sums=None):
+def attend(tiles, routed, names, cluster_tiles, last_tile_pad, own, sibling, held, sums=None, late=False):
     early = sums is None
     chosen = [i for i, step in enumerate(STEPS) if step[0] in names]
     rows = tuple(routed[1][i] for i in chosen)
     width = own.shape[1]
     flat = jnp.array([routed[2][i][d] for d in range(tiles) for i in chosen], jnp.int32)
-    bounds = (4, 8)
+    bounds = (4, 8) if early else (4,)
     base = TILE if early else 2 * TILE
     assert bounds[-1] * HALF >= sum(rows) + TILE * early
     smem = pl.BlockSpec(memory_space=pltpu.SMEM)
     anywhere = pl.BlockSpec(memory_space=pl.ANY)
     vmem = pl.BlockSpec(memory_space=pltpu.VMEM)
-    if early:
+    if not late:
         outs = (jax.ShapeDtypeStruct((TILE, width + 2 * TILE), jnp.float32),) * 2
     else:
         outs = tuple(jax.ShapeDtypeStruct((TILE, width + TILE), kind) for kind in (jnp.float32, jnp.bfloat16))
     columns = sum(rows) + TILE * early
     return pl.pallas_call(
-        functools.partial(attend_kernel, rows, bounds, cluster_tiles.shape[0], early),
+        functools.partial(attend_kernel, rows, bounds, cluster_tiles.shape[0], early, late),
         out_shape=outs,
         in_specs=[smem] * 3 + [anywhere] * (2 + len(rows)) + [vmem] * (0 if early else 2),
         out_specs=(vmem, vmem),
@@ -280,6 +283,8 @@
 
 
 FIRST = ("a", "b", "y")
+SECOND = ("w0", "w1", "s")
+THIRD = ("x", "r0", "r1")
 
 
 def body(embeddings, cluster_tiles, last_tile_pad):
@@ -305,20 +310,27 @@
     for name in FIRST:
         send(name)
     held["sib"] = lax.ppermute(embeddings, "tiles", cores)
-    together("sib", "b", "y", "a")
+    together("a", "y")
     send("w0")
     send("x")
+    together("sib", "b")
     me = lax.axis_index("tiles")
     held["ab"] = jnp.where(me % 2 == me // 2 % 2, held["a"], held["b"])
     send("s")
-    together("a", "w0")
-    for name in ("r0", "w1", "r1"):
-        send(name)
-    sibling = held["sib"]
-    common = (cluster_tiles, last_tile_pad, embeddings, sibling, held)
-    sums = attend(tiles, routed, FIRST, *common)
-    rest = [step[0] for step in STEPS if step[0] not in FIRST]
-    own_sum, sib_sum = attend(tiles, routed, rest, *common, sums)
+
+    def added(names, **more):
+        return attend(
+            tiles, routed, names, cluster_tiles, last_tile_pad, embeddings, held["sib"], held, **more
+        )
+
+    held["own_sum"], held["sib_sum"] = added(FIRST)
+    together("a", "w0", "own_sum", "sib_sum")
+    send("w1")
+    send("r0")
+    together("s", "w1")
+    send("r1")
+    sums = added(SECOND, sums=(held["own_sum"], held["sib_sum"]))
+    own_sum, sib_sum = added(THIRD, sums=sums, late=True)
     other_sum = lax.ppermute(sib_sum, "tiles", cores)
     numer = own_sum[:, :width] + other_sum[:, :width].astype(jnp.float32)
     parts = other_sum[:, width : width + 3].astype(jnp.float32)

time: 84.4 us -> 81.9 us (0.970)
  the two profiles are of different devices: /device:TPU:0 before, /device:TPU:17 now
where the time goes in v3:
time: 81.9 us; the launch traced here: 81.1 us
  waiting for transfers between devices  37.2 us (45%)
  starting transfers between devices  26.1 us (32%)
  Pallas kernels  15.6 us (19%)
  other arithmetic  1.79 us (2%)
    ppermute x9, waiting for transfers between devices, send(): held[name] = lax.ppermute(operand, 'tiles', pairs[name])  34.9 us
    ppermute x9, starting transfers between devices, send(): held[name] = lax.ppermute(operand, 'tiles', pairs[name])  20.9 us
    pallas_call x3, Pallas kernels, attend(): pl.pallas_call(functools.partial(attend_kernel, rows, bounds, cluster_til...  15.6 us
    ppermute x1, starting transfers between devices, body(): other_sum = lax.ppermute(sib_sum, 'tiles', cores)  3.62 us
    ppermute x1, waiting for transfers between devices, body(): other_sum = lax.ppermute(sib_sum, 'tiles', cores)  2.33 us
  transfers between devices with their start and end apart: 11, of which 7 were waited for; matrix products, arithmetic and copies ran while one was open for 0% of the time, Pallas kernels for 14%

profile of v3, /device:TPU:17, one launch (start us, length us, event | category | flops | bytes accessed | tf_op | source)
XLA Modules:
  0.0 81.1 jit_solution(4368113132645287644)
XLA Ops:
  0.0 1.2 %collective-permute-start.3 = (bf16[128,4096]{1,0:T(8,128)(2,1)}, bf16[128,4096]{1,0:T(8,128)(2,1)}, u32[]{:S(2)}, u32[]{:S(2)}) collective-permute-start(bf16[128,4096]{1,0:T(8,128)(2,1)} %rest_0_.5), channel_id=1, source_target_pairs={{0,2},{1,3},{2,0},{3,1},{4,6},{5,7},{6,4},{7,5},{8,10},{9,11},{10,... | collective-permute-start | bytes 3145736 | tf_op jit(solution)/shard_map/ppermute | solution.py:305
  1.2 2.1 %collective-permute-start.2 = (bf16[128,4096]{1,0:T(8,128)(2,1)}, bf16[128,4096]{1,0:T(8,128)(2,1)S(1)}, u32[]{:S(2)}, u32[]{:S(2)}) collective-permute-start(bf16[128,4096]{1,0:T(8,128)(2,1)} %rest_0_.5), channel_id=1, source_target_pairs={{2,6},{3,7},{4,0},{5,1},{6,10},{7,11},{8,4},{9,5},{10,14},{11,15},... | collective-permute-start | bytes 3145736 | tf_op jit(solution)/shard_map/ppermute | solution.py:305
  3.3 3.3 %collective-permute-start.1 = (bf16[128,4096]{1,0:T(8,128)(2,1)}, bf16[128,4096]{1,0:T(8,128)(2,1)S(1)}, u32[]{:S(2)}, u32[]{:S(2)}) collective-permute-start(bf16[128,4096]{1,0:T(8,128)(2,1)} %rest_0_.5), channel_id=1, source_target_pairs={{0,4},{1,5},{4,8},{5,9},{6,2},{7,3},{8,12},{9,13},{10,6},{11,7},{1... | collective-permute-start | bytes 3145736 | tf_op jit(solution)/shard_map/ppermute | solution.py:305
  6.6 1.6 %collective-permute-start = (bf16[128,4096]{1,0:T(8,128)(2,1)}, bf16[128,4096]{1,0:T(8,128)(2,1)S(1)}, u32[]{:S(2)}, u32[]{:S(2)}) collective-permute-start(bf16[128,4096]{1,0:T(8,128)(2,1)} %rest_0_.5), channel_id=1, source_target_pairs={{0,1},{1,0},{2,3},{3,2},{4,5},{5,4},{6,7},{7,6},{8,9},{9,8},{10,11... | collective-permute-start | bytes 3145736 | tf_op jit(solution)/shard_map/ppermute | solution.py:312
  8.2 16.2 %collective-permute-done.3.rest_4_ = bf16[128,4096]{1,0:T(8,128)(2,1)} collective-permute-done((bf16[128,4096]{1,0:T(8,128)(2,1)}, bf16[128,4096]{1,0:T(8,128)(2,1)}, u32[]{:S(2)}, u32[]{:S(2)}) %collective-permute-start.3) | collective-permute-done | bytes 1048608 | tf_op jit(solution)/shard_map/ppermute | solution.py:305
  24.3 2.7 %collective-permute-done.2.rest_2_ = bf16[128,4096]{1,0:T(8,128)(2,1)S(1)} collective-permute-done((bf16[128,4096]{1,0:T(8,128)(2,1)}, bf16[128,4096]{1,0:T(8,128)(2,1)S(1)}, u32[]{:S(2)}, u32[]{:S(2)}) %collective-permute-start.2) | collective-permute-done | bytes 1048608 | tf_op jit(solution)/shard_map/ppermute | solution.py:305
  27.1 2.1 %collective-permute-start.5 = (bf16[64,4096]{1,0:T(8,128)(2,1)S(1)}, bf16[64,4096]{1,0:T(8,128)(2,1)S(1)}, u32[]{:S(2)}, u32[]{:S(2)}) collective-permute-start(bf16[64,4096]{1,0:T(8,128)(2,1)S(1)} %slice.27), channel_id=1, source_target_pairs={{0,2},{1,3},{4,6},{5,7},{6,4},{7,5},{8,10},{9,11},{10,8},{11,9},{1... | collective-permute-start | bytes 1572872 | tf_op jit(solution)/shard_map/ppermute | solution.py:305
  29.2 0.0 collective-permute-done.1.rest_3_
  29.2 0.0 collective-permute-done.rest_1_
  29.2 0.1 broadcast_select_fusion
  29.4 0.0 copy-start.4
  29.4 2.9 %collective-permute-start.7 = (bf16[128,4096]{1,0:T(8,128)(2,1)S(1)}, bf16[128,4096]{1,0:T(8,128)(2,1)S(1)}, u32[]{:S(2)}, u32[]{:S(2)}) collective-permute-start(bf16[128,4096]{1,0:T(8,128)(2,1)S(1)} %broadcast_select_fusion), channel_id=1, source_target_pairs={{4,0},{5,9},{6,2},{7,11},{8,4},{9,13},{10,6},{11,15},{20,16},{21,2... | collective-permute-start | bytes 3145736 | tf_op jit(solution)/shard_map/ppermute | solution.py:305
  32.2 0.0 copy-done
  32.3 7.5 %shard_map.64 = (f32[128,4352]{1,0:T(8,128)S(1)}, f32[128,4352]{1,0:T(8,128)S(1)}) custom-call(s32[6]{0:T(128)S(1)} %copy-done.1, s32[6]{0:T(128)S(1)} %copy-done.2, s32[48]{0:T(128)S(1)} %copy-done.5, bf16[128,4096]{1,0:T(8,128)(2,1)S(1)} %copy-done, bf16[128,4096]{1,0:T(8,128)(2,1)S(1)} %collective-permute-done.rest_1_, ...), custom_call_target="tpu_custom_call" | custom-call | flops 2147483648 | bytes 6291456 | tf_op jit(solution)/shard_map/pallas_call | solution.py:266
  39.8 0.7 collective-permute-done.5.rest_2_
  40.6 0.0 copy-start.3
  40.6 2.1 %collective-permute-start.8 = (bf16[64,4096]{1,0:T(8,128)(2,1)S(1)}, bf16[64,4096]{1,0:T(8,128)(2,1)S(1)}, u32[]{:S(2)}, u32[]{:S(2)}) collective-permute-start(bf16[64,4096]{1,0:T(8,128)(2,1)S(1)} %slice.28), channel_id=1, source_target_pairs={{0,2},{1,3},{4,6},{5,7},{6,4},{7,5},{8,10},{9,11},{10,8},{11,9},{1... | collective-permute-start | bytes 1572872 | tf_op jit(solution)/shard_map/ppermute | solution.py:305
  42.7 2.8 %collective-permute-start.4 = (bf16[128,4096]{1,0:T(8,128)(2,1)}, bf16[128,4096]{1,0:T(8,128)(2,1)S(1)}, u32[]{:S(2)}, u32[]{:S(2)}) collective-permute-start(bf16[128,4096]{1,0:T(8,128)(2,1)} %collective-permute-done.3.rest_4_), channel_id=1, source_target_pairs={{2,6},{3,7},{4,0},{5,1},{6,10},{7,11},{8,4},{9,5},{10,14},{11,15},... | collective-permute-start | bytes 3145736 | tf_op jit(solution)/shard_map/ppermute | solution.py:305
  45.5 2.6 %collective-permute-start.6 = (bf16[64,4096]{1,0:T(8,128)(2,1)S(1)}, bf16[64,4096]{1,0:T(8,128)(2,1)S(1)}, u32[]{:S(2)}, u32[]{:S(2)}) collective-permute-start(bf16[64,4096]{1,0:T(8,128)(2,1)S(1)} %collective-permute-done.5.rest_2_), channel_id=1, source_target_pairs={{4,8},{5,9},{6,2},{7,3},{8,12},{9,13},{10,6},{11,7},{20,24},{21,25... | collective-permute-start | bytes 1572872 | tf_op jit(solution)/shard_map/ppermute | solution.py:305
  48.1 0.0 collective-permute-done.7.rest_4_
  48.1 5.0 %collective-permute-done.8.rest_3_ = bf16[64,4096]{1,0:T(8,128)(2,1)S(1)} collective-permute-done((bf16[64,4096]{1,0:T(8,128)(2,1)S(1)}, bf16[64,4096]{1,0:T(8,128)(2,1)S(1)}, u32[]{:S(2)}, u32[]{:S(2)}) %collective-permute-start.8) | collective-permute-done | bytes 524320 | tf_op jit(solution)/shard_map/ppermute | solution.py:305
  53.1 1.9 %collective-permute-start.9 = (bf16[64,4096]{1,0:T(8,128)(2,1)S(1)}, bf16[64,4096]{1,0:T(8,128)(2,1)S(1)}, u32[]{:S(2)}, u32[]{:S(2)}) collective-permute-start(bf16[64,4096]{1,0:T(8,128)(2,1)S(1)} %collective-permute-done.8.rest_3_), channel_id=1, source_target_pairs={{4,8},{5,9},{6,2},{7,3},{8,12},{9,13},{10,6},{11,7},{20,24},{21,25... | collective-permute-start | bytes 1572872 | tf_op jit(solution)/shard_map/ppermute | solution.py:305
  55.0 4.1 %shard_map.65 = (f32[128,4352]{1,0:T(8,128)S(1)}, f32[128,4352]{1,0:T(8,128)S(1)}) custom-call(s32[6]{0:T(128)S(1)} %copy-done.1, s32[6]{0:T(128)S(1)} %copy-done.2, s32[48]{0:T(128)S(1)} %copy-done.4, bf16[128,4096]{1,0:T(8,128)(2,1)S(1)} %copy-done, bf16[128,4096]{1,0:T(8,128)(2,1)S(1)} %collective-permute-done.rest_1_, ...), custom_call_target="tpu_custom_call" | custom-call | flops 1073741824 | bytes 4194304 | tf_op jit(solution)/shard_map/pallas_call | solution.py:266
  59.1 7.3 %collective-permute-done.4.rest_2_ = bf16[128,4096]{1,0:T(8,128)(2,1)S(1)} collective-permute-done((bf16[128,4096]{1,0:T(8,128)(2,1)}, bf16[128,4096]{1,0:T(8,128)(2,1)S(1)}, u32[]{:S(2)}, u32[]{:S(2)}) %collective-permute-start.4) | collective-permute-done | bytes 1048608 | tf_op jit(solution)/shard_map/ppermute | solution.py:305
  66.4 0.0 collective-permute-done.6.rest_3_
  66.4 3.0 %collective-permute-done.9.rest_4_ = bf16[64,4096]{1,0:T(8,128)(2,1)S(1)} collective-permute-done((bf16[64,4096]{1,0:T(8,128)(2,1)S(1)}, bf16[64,4096]{1,0:T(8,128)(2,1)S(1)}, u32[]{:S(2)}, u32[]{:S(2)}) %collective-permute-start.9) | collective-permute-done | bytes 524320 | tf_op jit(solution)/shard_map/ppermute | solution.py:305
  69.4 4.0 %shard_map.66 = (f32[128,4224]{1,0:T(8,128)S(1)}, bf16[128,4224]{1,0:T(8,128)(2,1)S(1)}) custom-call(s32[6]{0:T(128)S(1)} %copy-done.1, s32[6]{0:T(128)S(1)} %copy-done.2, s32[48]{0:T(128)S(1)} %copy-done.3, bf16[128,4096]{1,0:T(8,128)(2,1)S(1)} %copy-done, bf16[128,4096]{1,0:T(8,128)(2,1)S(1)} %collective-permute-done.rest_1_, ...), custom_call_target="tpu_custom_call" | custom-call | flops 1073741824 | bytes 4194304 | tf_op jit(solution)/shard_map/pallas_call | solution.py:266
  73.5 3.6 %collective-permute-start.10 = (bf16[128,4224]{1,0:T(8,128)(2,1)S(1)}, bf16[128,4224]{1,0:T(8,128)(2,1)S(1)}, u32[]{:S(2)}, u32[]{:S(2)}) collective-permute-start(bf16[128,4224]{1,0:T(8,128)(2,1)S(1)} %get-tuple-element.36), channel_id=1, source_target_pairs={{0,1},{1,0},{2,3},{3,2},{4,5},{5,4},{6,7},{7,6},{8,9},{9,8},{10,11... | collective-permute-start | bytes 3244040 | tf_op jit(solution)/shard_map/ppermute | solution.py:334
  77.1 2.3 %collective-permute-done.10 = bf16[128,4224]{1,0:T(8,128)(2,1)S(1)} collective-permute-done((bf16[128,4224]{1,0:T(8,128)(2,1)S(1)}, bf16[128,4224]{1,0:T(8,128)(2,1)S(1)}, u32[]{:S(2)}, u32[]{:S(2)}) %collective-permute-start.10) | collective-permute-done | bytes 1081376 | tf_op jit(solution)/shard_map/ppermute | solution.py:334
  79.4 0.2 compare_reduce_fusion
  79.6 0.1 fusion
  79.7 1.4 %select_convert_fusion = bf16[128,4096]{1,0:T(8,128)(2,1)} fusion(f32[128,4224]{1,0:T(8,128)S(1)} %get-tuple-element.35, bf16[128,4224]{1,0:T(8,128)(2,1)S(1)} %collective-permute-done.10, f32[128]{0:T(128)S(1)} %fusion, pred[128]{0:T(512)(128)(4,1)S(1)} %get-tuple-element.37), kind=kLoop, calls=%fused_computation | loop fusion | flops 2621440 | bytes 4194944 | tf_op jit(solution)/shard_map/convert_element_type | solution.py:339
  (12 shorter events, 0.1 us)
Async XLA Ops:
  0.0 24.3 %collective-permute-start.3 = (bf16[128,4096]{1,0:T(8,128)(2,1)}, bf16[128,4096]{1,0:T(8,128)(2,1)}, u32[]{:S(2)}, u32[]{:S(2)}) collective-permute-start(bf16[128,4096]{1,0:T(8,128)(2,1)} %rest_0_.5), channel_id=1, source_target_pairs={{0,2},{1,3},{2,0},{3,1},{4,6},{5,7},{6,4},{7,5},{8,10},{9,11},{10,... | collective-permute-start | bytes 3145736 | tf_op jit(solution)/shard_map/ppermute | solution.py:305
  1.2 25.8 %collective-permute-start.2 = (bf16[128,4096]{1,0:T(8,128)(2,1)}, bf16[128,4096]{1,0:T(8,128)(2,1)S(1)}, u32[]{:S(2)}, u32[]{:S(2)}) collective-permute-start(bf16[128,4096]{1,0:T(8,128)(2,1)} %rest_0_.5), channel_id=1, source_target_pairs={{2,6},{3,7},{4,0},{5,1},{6,10},{7,11},{8,4},{9,5},{10,14},{11,15},... | collective-permute-start | bytes 3145736 | tf_op jit(solution)/shard_map/ppermute | solution.py:305
  3.3 25.9 %collective-permute-start.1 = (bf16[128,4096]{1,0:T(8,128)(2,1)}, bf16[128,4096]{1,0:T(8,128)(2,1)S(1)}, u32[]{:S(2)}, u32[]{:S(2)}) collective-permute-start(bf16[128,4096]{1,0:T(8,128)(2,1)} %rest_0_.5), channel_id=1, source_target_pairs={{0,4},{1,5},{4,8},{5,9},{6,2},{7,3},{8,12},{9,13},{10,6},{11,7},{1... | collective-permute-start | bytes 3145736 | tf_op jit(solution)/shard_map/ppermute | solution.py:305
  6.6 22.6 %collective-permute-start = (bf16[128,4096]{1,0:T(8,128)(2,1)}, bf16[128,4096]{1,0:T(8,128)(2,1)S(1)}, u32[]{:S(2)}, u32[]{:S(2)}) collective-permute-start(bf16[128,4096]{1,0:T(8,128)(2,1)} %rest_0_.5), channel_id=1, source_target_pairs={{0,1},{1,0},{2,3},{3,2},{4,5},{5,4},{6,7},{7,6},{8,9},{9,8},{10,11... | collective-permute-start | bytes 3145736 | tf_op jit(solution)/shard_map/ppermute | solution.py:312
  8.2 24.1 %copy-start = (bf16[128,4096]{1,0:T(8,128)(2,1)S(1)}, bf16[128,4096]{1,0:T(8,128)(2,1)}, u32[]{:S(2)}) copy-start(bf16[128,4096]{1,0:T(8,128)(2,1)} %rest_0_.5) | copy-start | bytes 3145732
  8.2 24.1 %copy-start.1 = (s32[6]{0:T(128)S(1)}, s32[6]{0:T(128)}, u32[]{:S(2)}) copy-start(s32[6]{0:T(128)} %tiles_ref.5) | copy-start | bytes 76
  8.2 24.1 %copy-start.2 = (s32[6]{0:T(128)S(1)}, s32[6]{0:T(128)}, u32[]{:S(2)}) copy-start(s32[6]{0:T(128)} %pad_ref.5) | copy-start | bytes 76
  8.2 24.1 %copy-start.5 = (s32[48]{0:T(128)S(1)}, s32[48]{0:T(128)}, u32[]{:S(2)}) copy-start(s32[48]{0:T(128)} %constant.43.clone.table_ref) | copy-start | bytes 580
  27.1 13.4 %collective-permute-start.5 = (bf16[64,4096]{1,0:T(8,128)(2,1)S(1)}, bf16[64,4096]{1,0:T(8,128)(2,1)S(1)}, u32[]{:S(2)}, u32[]{:S(2)}) collective-permute-start(bf16[64,4096]{1,0:T(8,128)(2,1)S(1)} %slice.27), channel_id=1, source_target_pairs={{0,2},{1,3},{4,6},{5,7},{6,4},{7,5},{8,10},{9,11},{10,8},{11,9},{1... | collective-permute-start | bytes 1572872 | tf_op jit(solution)/shard_map/ppermute | solution.py:305
  29.4 25.7 %copy-start.4 = (s32[48]{0:T(128)S(1)}, s32[48]{0:T(128)}, u32[]{:S(2)}) copy-start(s32[48]{0:T(128)} %constant.44.clone.table_ref) | copy-start | bytes 580
  29.4 18.7 %collective-permute-start.7 = (bf16[128,4096]{1,0:T(8,128)(2,1)S(1)}, bf16[128,4096]{1,0:T(8,128)(2,1)S(1)}, u32[]{:S(2)}, u32[]{:S(2)}) collective-permute-start(bf16[128,4096]{1,0:T(8,128)(2,1)S(1)} %broadcast_select_fusion), channel_id=1, source_target_pairs={{4,0},{5,9},{6,2},{7,11},{8,4},{9,13},{10,6},{11,15},{20,16},{21,2... | collective-permute-start | bytes 3145736 | tf_op jit(solution)/shard_map/ppermute | solution.py:305
  40.6 28.9 %copy-start.3 = (s32[48]{0:T(128)S(1)}, s32[48]{0:T(128)}, u32[]{:S(2)}) copy-start(s32[48]{0:T(128)} %constant.45.clone.table_ref) | copy-start | bytes 580
  40.6 12.5 %collective-permute-start.8 = (bf16[64,4096]{1,0:T(8,128)(2,1)S(1)}, bf16[64,4096]{1,0:T(8,128)(2,1)S(1)}, u32[]{:S(2)}, u32[]{:S(2)}) collective-permute-start(bf16[64,4096]{1,0:T(8,128)(2,1)S(1)} %slice.28), channel_id=1, source_target_pairs={{0,2},{1,3},{4,6},{5,7},{6,4},{7,5},{8,10},{9,11},{10,8},{11,9},{1... | collective-permute-start | bytes 1572872 | tf_op jit(solution)/shard_map/ppermute | solution.py:305
  42.7 23.7 %collective-permute-start.4 = (bf16[128,4096]{1,0:T(8,128)(2,1)}, bf16[128,4096]{1,0:T(8,128)(2,1)S(1)}, u32[]{:S(2)}, u32[]{:S(2)}) collective-permute-start(bf16[128,4096]{1,0:T(8,128)(2,1)} %collective-permute-done.3.rest_4_), channel_id=1, source_target_pairs={{2,6},{3,7},{4,0},{5,1},{6,10},{7,11},{8,4},{9,5},{10,14},{11,15},... | collective-permute-start | bytes 3145736 | tf_op jit(solution)/shard_map/ppermute | solution.py:305
  45.5 20.9 %collective-permute-start.6 = (bf16[64,4096]{1,0:T(8,128)(2,1)S(1)}, bf16[64,4096]{1,0:T(8,128)(2,1)S(1)}, u32[]{:S(2)}, u32[]{:S(2)}) collective-permute-start(bf16[64,4096]{1,0:T(8,128)(2,1)S(1)} %collective-permute-done.5.rest_2_), channel_id=1, source_target_pairs={{4,8},{5,9},{6,2},{7,3},{8,12},{9,13},{10,6},{11,7},{20,24},{21,25... | collective-permute-start | bytes 1572872 | tf_op jit(solution)/shard_map/ppermute | solution.py:305
  53.1 16.3 %collective-permute-start.9 = (bf16[64,4096]{1,0:T(8,128)(2,1)S(1)}, bf16[64,4096]{1,0:T(8,128)(2,1)S(1)}, u32[]{:S(2)}, u32[]{:S(2)}) collective-permute-start(bf16[64,4096]{1,0:T(8,128)(2,1)S(1)} %collective-permute-done.8.rest_3_), channel_id=1, source_target_pairs={{4,8},{5,9},{6,2},{7,3},{8,12},{9,13},{10,6},{11,7},{20,24},{21,25... | collective-permute-start | bytes 1572872 | tf_op jit(solution)/shard_map/ppermute | solution.py:305
  73.5 6.0 %collective-permute-start.10 = (bf16[128,4224]{1,0:T(8,128)(2,1)S(1)}, bf16[128,4224]{1,0:T(8,128)(2,1)S(1)}, u32[]{:S(2)}, u32[]{:S(2)}) collective-permute-start(bf16[128,4224]{1,0:T(8,128)(2,1)S(1)} %get-tuple-element.36), channel_id=1, source_target_pairs={{0,1},{1,0},{2,3},{3,2},{4,5},{5,4},{6,7},{7,6},{8,9},{9,8},{10,11... | collective-permute-start | bytes 3244040 | tf_op jit(solution)/shard_map/ppermute | solution.py:334

commit v4 on v3

--- a/solution.py
+++ b/solution.py
@@ -79,6 +79,17 @@
     return pairs, rows, table
 
 
+def tile_layout(clusters, tiles_ref, pad_ref, tile):
+    start, cluster, live = jnp.int32(0), jnp.int32(-1), jnp.int32(0)
+    for c in range(clusters):
+        count = tiles_ref[c]
+        inside = (start <= tile) & (tile < start + count)
+        cluster = jnp.where(inside, c, cluster)
+        live = jnp.where(inside, count * TILE - pad_ref[c] - (tile - start) * TILE, live)
+        start = start + count
+    return cluster, jnp.clip(live, 0, TILE)
+
+
 def attend_kernel(rows, bounds, clusters, early, late, tiles_ref, pad_ref, table_ref, *rest):
     own_ref, sib_ref = rest[:2]
     pieces = rest[2 : 2 + len(rows)]
@@ -86,22 +97,15 @@
     if not early:
         own_in, sib_in = rest[:2]
         rest = rest[2:]
+    if late:
+        weights_out, rest = rest[0], rest[1:]
     own_out, sib_out, held, weights, limits, den, sems = rest
     width = own_ref.shape[1]
     me = lax.axis_index("tiles")
     other = me + 1 - 2 * lax.rem(me, 2)
     base = TILE if early else 2 * TILE
 
-    def layout(tile):
-        start, cluster, live = jnp.int32(0), jnp.int32(-1), jnp.int32(0)
-        for c in range(clusters):
-            count = tiles_ref[c]
-            inside = (start <= tile) & (tile < start + count)
-            cluster = jnp.where(inside, c, cluster)
-            live = jnp.where(inside, count * TILE - pad_ref[c] - (tile - start) * TILE, live)
-            start = start + count
-        return cluster, jnp.clip(live, 0, TILE)
-
+    layout = functools.partial(tile_layout, clusters, tiles_ref, pad_ref)
     copies = [
         pltpu.make_async_copy(sib_ref, held.at[pl.ds(0, TILE)], sems.at[0]),
         pltpu.make_async_copy(own_ref, held.at[pl.ds(TILE, TILE)], sems.at[1]),
@@ -217,14 +221,17 @@
         def _(f):
             at = pl.ds(pl.multiple_of(f * chunk, chunk), chunk)
             total = jnp.dot(
-                weights[:, pl.ds(0, depth)], held[pl.ds(base, depth), at], preferred_element_type=jnp.float32
+                weights[pl.ds(0, TILE if late else 2 * TILE), pl.ds(0, depth)],
+                held[pl.ds(base, depth), at],
+                preferred_element_type=jnp.float32,
             )
             if early:
                 sib_out[:, at] = total[:TILE]
                 own_out[:, at] = total[TILE:]
             else:
                 sib_out[:, at] = (sib_in[:, at] + total[:TILE]).astype(sib_out.dtype)
-                own_out[:, at] = own_in[:, at] + total[TILE:]
+                if not late:
+                    own_out[:, at] = own_in[:, at] + total[TILE:]
 
     for depth in bounds:
 
@@ -232,7 +239,9 @@
         def _(depth=depth):
             products(depth * HALF)
 
-    own_out[:, pl.ds(width, TILE)] = den[pl.ds(TILE, TILE), :]
+    if late:
+        weights_out[...] = weights[pl.ds(TILE, TILE), :]
+    own_out[:, pl.ds(0 if late else width, TILE)] = den[pl.ds(TILE, TILE), :]
     whole = den[pl.ds(0, TILE), :]
     if not late:
         sib_out[:, pl.ds(width, TILE)] = whole
@@ -261,13 +270,17 @@
     if not late:
         outs = (jax.ShapeDtypeStruct((TILE, width + 2 * TILE), jnp.float32),) * 2
     else:
-        outs = tuple(jax.ShapeDtypeStruct((TILE, width + TILE), kind) for kind in (jnp.float32, jnp.bfloat16))
+        outs = (
+            jax.ShapeDtypeStruct((TILE, bounds[-1] * HALF), jnp.bfloat16),
+            jax.ShapeDtypeStruct((TILE, TILE), jnp.float32),
+            jax.ShapeDtypeStruct((TILE, width + TILE), jnp.bfloat16),
+        )
     columns = sum(rows) + TILE * early
     return pl.pallas_call(
         functools.partial(attend_kernel, rows, bounds, cluster_tiles.shape[0], early, late),
         out_shape=outs,
         in_specs=[smem] * 3 + [anywhere] * (2 + len(rows)) + [vmem] * (0 if early else 2),
-        out_specs=(vmem, vmem),
+        out_specs=(vmem,) * len(outs),
         scratch_shapes=[
             pltpu.VMEM((base + bounds[-1] * HALF, width), jnp.bfloat16),
             pltpu.VMEM((2 * TILE, bounds[-1] * HALF), jnp.bfloat16),
@@ -282,6 +295,73 @@
     )(cluster_tiles, last_tile_pad, flat, own, sibling, *[held[STEPS[i][0]] for i in chosen], *(sums or ()))
 
 
+def own_kernel(rows, units, clusters, tiles_ref, pad_ref, table_ref, *rest):
+    pieces = rest[: len(rows)]
+    weights_in, own_in, own_out, held, sems = rest[len(rows) :]
+    width = own_out.shape[1]
+    me = lax.axis_index("tiles")
+    layout = functools.partial(tile_layout, clusters, tiles_ref, pad_ref)
+    own_cluster, _ = layout(me)
+    sib_cluster, _ = layout(me + 1 - 2 * lax.rem(me, 2))
+    used = jnp.int32(0)
+    pending = []
+    for i, count in enumerate(rows):
+        piece = table_ref[me * len(rows) + i]
+        cluster, _ = layout(lax.shift_right_arithmetic(piece, 1))
+        valid = (piece >= 0) & ((cluster == own_cluster) | (cluster == sib_cluster))
+        place = pl.multiple_of(used * HALF, HALF)
+        copy = pltpu.make_async_copy(pieces[i], held.at[pl.ds(place, count)], sems.at[i])
+
+        @pl.when(valid)
+        def _(copy=copy):
+            copy.start()
+
+        pending.append((valid, copy))
+        used = used + jnp.where(valid, count // HALF, 0)
+    for unit in range(units):
+
+        @pl.when(unit >= used)
+        def _(unit=unit):
+            held[pl.ds(unit * HALF, HALF), :] = jnp.zeros((HALF, width), held.dtype)
+
+    for valid, copy in pending:
+
+        @pl.when(valid)
+        def _(copy=copy):
+            copy.wait()
+
+    chunk = 512
+
+    @pl.loop(0, width // chunk)
+    def _(f):
+        at = pl.ds(pl.multiple_of(f * chunk, chunk), chunk)
+        own_out[:, at] = own_in[:, at] + jnp.dot(weights_in[...], held[:, at], preferred_element_type=jnp.float32)
+
+
+def own_products(tiles, routed, names, cluster_tiles, last_tile_pad, held, weights, own_sum):
+    chosen = [i for i, step in enumerate(STEPS) if step[0] in names]
+    rows = tuple(routed[1][i] for i in chosen)
+    depth, width = weights.shape[1], own_sum.shape[1] - 2 * TILE
+    flat = jnp.array([routed[2][i][d] for d in range(tiles) for i in chosen], jnp.int32)
+    assert sum(rows) <= depth
+    smem = pl.BlockSpec(memory_space=pltpu.SMEM)
+    vmem = pl.BlockSpec(memory_space=pltpu.VMEM)
+    return pl.pallas_call(
+        functools.partial(own_kernel, rows, depth // HALF, cluster_tiles.shape[0]),
+        out_shape=jax.ShapeDtypeStruct((TILE, width), jnp.float32),
+        in_specs=[smem] * 3 + [pl.BlockSpec(memory_space=pl.ANY)] * len(rows) + [vmem] * 2,
+        out_specs=vmem,
+        scratch_shapes=[
+            pltpu.VMEM((depth, width), jnp.bfloat16),
+            pltpu.SemaphoreType.DMA((len(rows),)),
+        ],
+        compiler_params=pltpu.CompilerParams(vmem_limit_bytes=32 * 1024 * 1024),
+        cost_estimate=pl.CostEstimate(
+            flops=2 * TILE * depth * width, bytes_accessed=2 * depth * width, transcendentals=0
+        ),
+    )(cluster_tiles, last_tile_pad, flat, *[held[STEPS[i][0]] for i in chosen], weights, own_sum)
+
+
 FIRST = ("a", "b", "y")
 SECOND = ("w0", "w1", "s")
 THIRD = ("x", "r0", "r1")
@@ -330,11 +410,12 @@
     together("s", "w1")
     send("r1")
     sums = added(SECOND, sums=(held["own_sum"], held["sib_sum"]))
-    own_sum, sib_sum = added(THIRD, sums=sums, late=True)
+    weights, own_den, sib_sum = added(THIRD, sums=sums, late=True)
     other_sum = lax.ppermute(sib_sum, "tiles", cores)
-    numer = own_sum[:, :width] + other_sum[:, :width].astype(jnp.float32)
+    own_sum = own_products(tiles, routed, THIRD, cluster_tiles, last_tile_pad, held, weights, sums[0])
+    numer = own_sum + other_sum[:, :width].astype(jnp.float32)
     parts = other_sum[:, width : width + 3].astype(jnp.float32)
-    denom = own_sum[:, width] + (parts[:, 0] + parts[:, 1] + parts[:, 2])
+    denom = own_den[:, 0] + (parts[:, 0] + parts[:, 1] + parts[:, 2])
     live = denom > 0.0
     return jnp.where(live[:, None], numer / jnp.where(live, denom, 1.0)[:, None], 0.0).astype(jnp.bfloat16)
 

time: 81.9 us -> 81.7 us (level)
  waiting for transfers between devices: 37.2 us -> 34.9 us
  Pallas kernels: 15.6 us -> 17.7 us
    pallas_call x0 -> x1, Pallas kernels: none -> 2.35 us  [own_products(): pl.pallas_call(functools.partial(own_kernel, rows, depth // HALF, cluster...]
    ppermute x1, waiting for transfers between devices: 2.33 us -> 0.01 us  [body(): other_sum = lax.ppermute(sib_sum, 'tiles', cores)]
  transfers between devices with their start and end apart: 11 -> 11, of which waited for: 7 -> 6; matrix products, arithmetic and copies ran while one was open for 0% -> 0% of each run, Pallas kernels for 14% -> 17%
where the time goes in v4:
time: 81.7 us; the launch traced here: 80.9 us
  waiting for transfers between devices  34.9 us (43%)
  starting transfers between devices  26.2 us (32%)
  Pallas kernels  17.7 us (22%)
  other arithmetic  1.8 us (2%)
    ppermute x9, waiting for transfers between devices, send(): held[name] = lax.ppermute(operand, 'tiles', pairs[name])  34.9 us
    ppermute x9, starting transfers between devices, send(): held[name] = lax.ppermute(operand, 'tiles', pairs[name])  20.9 us
    pallas_call x3, Pallas kernels, attend(): pl.pallas_call(functools.partial(attend_kernel, rows, bounds, cluster_til...  15.3 us
    ppermute x1, starting transfers between devices, body(): other_sum = lax.ppermute(sib_sum, 'tiles', cores)  3.63 us
    pallas_call x1, Pallas kernels, own_products(): pl.pallas_call(functools.partial(own_kernel, rows, depth // HALF, cluster...  2.35 us
  transfers between devices with their start and end apart: 11, of which 6 were waited for; matrix products, arithmetic and copies ran while one was open for 0% of the time, Pallas kernels for 17%

profile of v4, /device:TPU:17, one launch (start us, length us, event | category | flops | bytes accessed | tf_op | source)
XLA Modules:
  0.0 80.9 jit_solution(8209545361981925429)
XLA Ops:
  0.0 1.2 %collective-permute-start.3 = (bf16[128,4096]{1,0:T(8,128)(2,1)}, bf16[128,4096]{1,0:T(8,128)(2,1)}, u32[]{:S(2)}, u32[]{:S(2)}) collective-permute-start(bf16[128,4096]{1,0:T(8,128)(2,1)} %rest_0_.5), channel_id=1, source_target_pairs={{0,2},{1,3},{2,0},{3,1},{4,6},{5,7},{6,4},{7,5},{8,10},{9,11},{10,... | collective-permute-start | bytes 3145736 | tf_op jit(solution)/shard_map/ppermute | solution.py:385
  1.2 2.1 %collective-permute-start.2 = (bf16[128,4096]{1,0:T(8,128)(2,1)}, bf16[128,4096]{1,0:T(8,128)(2,1)S(1)}, u32[]{:S(2)}, u32[]{:S(2)}) collective-permute-start(bf16[128,4096]{1,0:T(8,128)(2,1)} %rest_0_.5), channel_id=1, source_target_pairs={{2,6},{3,7},{4,0},{5,1},{6,10},{7,11},{8,4},{9,5},{10,14},{11,15},... | collective-permute-start | bytes 3145736 | tf_op jit(solution)/shard_map/ppermute | solution.py:385
  3.3 3.3 %collective-permute-start.1 = (bf16[128,4096]{1,0:T(8,128)(2,1)}, bf16[128,4096]{1,0:T(8,128)(2,1)S(1)}, u32[]{:S(2)}, u32[]{:S(2)}) collective-permute-start(bf16[128,4096]{1,0:T(8,128)(2,1)} %rest_0_.5), channel_id=1, source_target_pairs={{0,4},{1,5},{4,8},{5,9},{6,2},{7,3},{8,12},{9,13},{10,6},{11,7},{1... | collective-permute-start | bytes 3145736 | tf_op jit(solution)/shard_map/ppermute | solution.py:385
  6.6 1.6 %collective-permute-start = (bf16[128,4096]{1,0:T(8,128)(2,1)}, bf16[128,4096]{1,0:T(8,128)(2,1)S(1)}, u32[]{:S(2)}, u32[]{:S(2)}) collective-permute-start(bf16[128,4096]{1,0:T(8,128)(2,1)} %rest_0_.5), channel_id=1, source_target_pairs={{0,1},{1,0},{2,3},{3,2},{4,5},{5,4},{6,7},{7,6},{8,9},{9,8},{10,11... | collective-permute-start | bytes 3145736 | tf_op jit(solution)/shard_map/ppermute | solution.py:392
  8.2 16.2 %collective-permute-done.3.rest_4_ = bf16[128,4096]{1,0:T(8,128)(2,1)} collective-permute-done((bf16[128,4096]{1,0:T(8,128)(2,1)}, bf16[128,4096]{1,0:T(8,128)(2,1)}, u32[]{:S(2)}, u32[]{:S(2)}) %collective-permute-start.3) | collective-permute-done | bytes 1048608 | tf_op jit(solution)/shard_map/ppermute | solution.py:385
  24.3 2.7 %collective-permute-done.2.rest_2_ = bf16[128,4096]{1,0:T(8,128)(2,1)S(1)} collective-permute-done((bf16[128,4096]{1,0:T(8,128)(2,1)}, bf16[128,4096]{1,0:T(8,128)(2,1)S(1)}, u32[]{:S(2)}, u32[]{:S(2)}) %collective-permute-start.2) | collective-permute-done | bytes 1048608 | tf_op jit(solution)/shard_map/ppermute | solution.py:385
  27.1 2.1 %collective-permute-start.5 = (bf16[64,4096]{1,0:T(8,128)(2,1)S(1)}, bf16[64,4096]{1,0:T(8,128)(2,1)S(1)}, u32[]{:S(2)}, u32[]{:S(2)}) collective-permute-start(bf16[64,4096]{1,0:T(8,128)(2,1)S(1)} %slice.24), channel_id=1, source_target_pairs={{0,2},{1,3},{4,6},{5,7},{6,4},{7,5},{8,10},{9,11},{10,8},{11,9},{1... | collective-permute-start | bytes 1572872 | tf_op jit(solution)/shard_map/ppermute | solution.py:385
  29.2 0.0 collective-permute-done.1.rest_3_
  29.2 0.0 collective-permute-done.rest_1_
  29.2 0.1 broadcast_select_fusion
  29.4 0.0 copy-start.4
  29.4 2.9 %collective-permute-start.7 = (bf16[128,4096]{1,0:T(8,128)(2,1)S(1)}, bf16[128,4096]{1,0:T(8,128)(2,1)S(1)}, u32[]{:S(2)}, u32[]{:S(2)}) collective-permute-start(bf16[128,4096]{1,0:T(8,128)(2,1)S(1)} %broadcast_select_fusion), channel_id=1, source_target_pairs={{4,0},{5,9},{6,2},{7,11},{8,4},{9,13},{10,6},{11,15},{20,16},{21,2... | collective-permute-start | bytes 3145736 | tf_op jit(solution)/shard_map/ppermute | solution.py:385
  32.3 7.5 %shard_map.73 = (f32[128,4352]{1,0:T(8,128)S(1)}, f32[128,4352]{1,0:T(8,128)S(1)}) custom-call(s32[6]{0:T(128)S(1)} %copy-done.1, s32[6]{0:T(128)S(1)} %copy-done.2, s32[48]{0:T(128)S(1)} %copy-done.5, bf16[128,4096]{1,0:T(8,128)(2,1)S(1)} %copy-done, bf16[128,4096]{1,0:T(8,128)(2,1)S(1)} %collective-permute-done.rest_1_, ...), custom_call_target="tpu_custom_call" | custom-call | flops 2147483648 | bytes 6291456 | tf_op jit(solution)/shard_map/pallas_call | solution.py:279
  39.8 0.7 collective-permute-done.5.rest_2_
  40.6 0.0 copy-start.3
  40.6 2.1 %collective-permute-start.8 = (bf16[64,4096]{1,0:T(8,128)(2,1)S(1)}, bf16[64,4096]{1,0:T(8,128)(2,1)S(1)}, u32[]{:S(2)}, u32[]{:S(2)}) collective-permute-start(bf16[64,4096]{1,0:T(8,128)(2,1)S(1)} %slice.25), channel_id=1, source_target_pairs={{0,2},{1,3},{4,6},{5,7},{6,4},{7,5},{8,10},{9,11},{10,8},{11,9},{1... | collective-permute-start | bytes 1572872 | tf_op jit(solution)/shard_map/ppermute | solution.py:385
  42.7 2.8 %collective-permute-start.4 = (bf16[128,4096]{1,0:T(8,128)(2,1)}, bf16[128,4096]{1,0:T(8,128)(2,1)S(1)}, u32[]{:S(2)}, u32[]{:S(2)}) collective-permute-start(bf16[128,4096]{1,0:T(8,128)(2,1)} %collective-permute-done.3.rest_4_), channel_id=1, source_target_pairs={{2,6},{3,7},{4,0},{5,1},{6,10},{7,11},{8,4},{9,5},{10,14},{11,15},... | collective-permute-start | bytes 3145736 | tf_op jit(solution)/shard_map/ppermute | solution.py:385
  45.5 2.6 %collective-permute-start.6 = (bf16[64,4096]{1,0:T(8,128)(2,1)S(1)}, bf16[64,4096]{1,0:T(8,128)(2,1)S(1)}, u32[]{:S(2)}, u32[]{:S(2)}) collective-permute-start(bf16[64,4096]{1,0:T(8,128)(2,1)S(1)} %collective-permute-done.5.rest_2_), channel_id=1, source_target_pairs={{4,8},{5,9},{6,2},{7,3},{8,12},{9,13},{10,6},{11,7},{20,24},{21,25... | collective-permute-start | bytes 1572872 | tf_op jit(solution)/shard_map/ppermute | solution.py:385
  48.1 0.0 collective-permute-done.7.rest_4_
  48.1 5.0 %collective-permute-done.8.rest_3_ = bf16[64,4096]{1,0:T(8,128)(2,1)S(1)} collective-permute-done((bf16[64,4096]{1,0:T(8,128)(2,1)S(1)}, bf16[64,4096]{1,0:T(8,128)(2,1)S(1)}, u32[]{:S(2)}, u32[]{:S(2)}) %collective-permute-start.8) | collective-permute-done | bytes 524320 | tf_op jit(solution)/shard_map/ppermute | solution.py:385
  53.1 1.9 %collective-permute-start.9 = (bf16[64,4096]{1,0:T(8,128)(2,1)S(1)}, bf16[64,4096]{1,0:T(8,128)(2,1)S(1)}, u32[]{:S(2)}, u32[]{:S(2)}) collective-permute-start(bf16[64,4096]{1,0:T(8,128)(2,1)S(1)} %collective-permute-done.8.rest_3_), channel_id=1, source_target_pairs={{4,8},{5,9},{6,2},{7,3},{8,12},{9,13},{10,6},{11,7},{20,24},{21,25... | collective-permute-start | bytes 1572872 | tf_op jit(solution)/shard_map/ppermute | solution.py:385
  55.0 4.1 %shard_map.74 = (f32[128,4352]{1,0:T(8,128)S(1)}, f32[128,4352]{1,0:T(8,128)S(1)}) custom-call(s32[6]{0:T(128)S(1)} %copy-done.1, s32[6]{0:T(128)S(1)} %copy-done.2, s32[48]{0:T(128)S(1)} %copy-done.4, bf16[128,4096]{1,0:T(8,128)(2,1)S(1)} %copy-done, bf16[128,4096]{1,0:T(8,128)(2,1)S(1)} %collective-permute-done.rest_1_, ...), custom_call_target="tpu_custom_call" | custom-call | flops 1073741824 | bytes 4194304 | tf_op jit(solution)/shard_map/pallas_call | solution.py:279
  59.1 7.3 %collective-permute-done.4.rest_2_.rest_0_ = bf16[128,4096]{1,0:T(8,128)(2,1)S(1)} collective-permute-done((bf16[128,4096]{1,0:T(8,128)(2,1)}, bf16[128,4096]{1,0:T(8,128)(2,1)S(1)}, u32[]{:S(2)}, u32[]{:S(2)}) %collective-permute-start.4) | collective-permute-done | bytes 1048608 | tf_op jit(solution)/shard_map/ppermute | solution.py:385
  66.4 0.0 collective-permute-done.6.rest_3_.rest_1_
  66.4 3.0 %collective-permute-done.9.rest_4_.rest_2_ = bf16[64,4096]{1,0:T(8,128)(2,1)S(1)} collective-permute-done((bf16[64,4096]{1,0:T(8,128)(2,1)S(1)}, bf16[64,4096]{1,0:T(8,128)(2,1)S(1)}, u32[]{:S(2)}, u32[]{:S(2)}) %collective-permute-start.9) | collective-permute-done | bytes 524320 | tf_op jit(solution)/shard_map/ppermute | solution.py:385
  69.4 3.7 %shard_map.75 = (bf16[128,256]{1,0:T(8,128)(2,1)S(1)}, f32[128,128]{1,0:T(8,128)S(1)}, bf16[128,4224]{1,0:T(8,128)(2,1)S(1)}) custom-call(s32[6]{0:T(128)S(1)} %copy-done.1, s32[6]{0:T(128)S(1)} %copy-done.2, s32[48]{0:T(128)S(1)} %copy-done.3, bf16[128,4096]{1,0:T(8,128)(2,1)S(1)} %copy-done, bf16[128,4096]{1,0:T(8,128)(2,1)S(1)} %collective-permute-done.rest_1_, ...), custom_call_target="tpu_custom_call" | custom-call | flops 1073741824 | bytes 4194304 | tf_op jit(solution)/shard_map/pallas_call | solution.py:279
  73.2 3.6 %collective-permute-start.10 = (bf16[128,4224]{1,0:T(8,128)(2,1)S(1)}, bf16[128,4224]{1,0:T(8,128)(2,1)S(1)}, u32[]{:S(2)}, u32[]{:S(2)}) collective-permute-start(bf16[128,4224]{1,0:T(8,128)(2,1)S(1)} %get-tuple-element.37), channel_id=1, source_target_pairs={{0,1},{1,0},{2,3},{3,2},{4,5},{5,4},{6,7},{7,6},{8,9},{9,8},{10,11... | collective-permute-start | bytes 3244040 | tf_op jit(solution)/shard_map/ppermute | solution.py:414
  76.8 2.4 %shard_map.76 = f32[128,4096]{1,0:T(8,128)S(1)} custom-call(s32[6]{0:T(128)S(1)} %copy-done.1, s32[6]{0:T(128)S(1)} %copy-done.2, s32[48]{0:T(128)S(1)} %copy-done.3, bf16[128,4096]{1,0:T(8,128)(2,1)S(1)} %collective-permute-done.4.rest_2_.rest_0_, bf16[64,4096]{1,0:T(8,128)(2,1)S(1)} %collective-permute-done.6.rest_3_.rest_1_, ...), custom_call_target="tpu_custom_call" | custom-call | flops 268435456 | bytes 2097152 | tf_op jit(solution)/shard_map/pallas_call | solution.py:349
  79.2 0.0 collective-permute-done.10
  79.2 0.2 compare_reduce_fusion
  79.4 0.1 fusion
  79.5 1.4 %select_convert_fusion = bf16[128,4096]{1,0:T(8,128)(2,1)} fusion(f32[128,4096]{1,0:T(8,128)S(1)} %shard_map.76, bf16[128,4224]{1,0:T(8,128)(2,1)S(1)} %collective-permute-done.10, f32[128]{0:T(128)S(1)} %fusion, pred[128]{0:T(512)(128)(4,1)S(1)} %get-tuple-element.39), kind=kLoop, calls=%fused_computation | loop fusion | flops 2621440 | bytes 4194944 | tf_op jit(solution)/shard_map/convert_element_type | solution.py:420
  (13 shorter events, 0.1 us)
Async XLA Ops:
  0.0 24.3 %collective-permute-start.3 = (bf16[128,4096]{1,0:T(8,128)(2,1)}, bf16[128,4096]{1,0:T(8,128)(2,1)}, u32[]{:S(2)}, u32[]{:S(2)}) collective-permute-start(bf16[128,4096]{1,0:T(8,128)(2,1)} %rest_0_.5), channel_id=1, source_target_pairs={{0,2},{1,3},{2,0},{3,1},{4,6},{5,7},{6,4},{7,5},{8,10},{9,11},{10,... | collective-permute-start | bytes 3145736 | tf_op jit(solution)/shard_map/ppermute | solution.py:385
  1.2 25.8 %collective-permute-start.2 = (bf16[128,4096]{1,0:T(8,128)(2,1)}, bf16[128,4096]{1,0:T(8,128)(2,1)S(1)}, u32[]{:S(2)}, u32[]{:S(2)}) collective-permute-start(bf16[128,4096]{1,0:T(8,128)(2,1)} %rest_0_.5), channel_id=1, source_target_pairs={{2,6},{3,7},{4,0},{5,1},{6,10},{7,11},{8,4},{9,5},{10,14},{11,15},... | collective-permute-start | bytes 3145736 | tf_op jit(solution)/shard_map/ppermute | solution.py:385
  3.3 25.9 %collective-permute-start.1 = (bf16[128,4096]{1,0:T(8,128)(2,1)}, bf16[128,4096]{1,0:T(8,128)(2,1)S(1)}, u32[]{:S(2)}, u32[]{:S(2)}) collective-permute-start(bf16[128,4096]{1,0:T(8,128)(2,1)} %rest_0_.5), channel_id=1, source_target_pairs={{0,4},{1,5},{4,8},{5,9},{6,2},{7,3},{8,12},{9,13},{10,6},{11,7},{1... | collective-permute-start | bytes 3145736 | tf_op jit(solution)/shard_map/ppermute | solution.py:385
  6.6 22.6 %collective-permute-start = (bf16[128,4096]{1,0:T(8,128)(2,1)}, bf16[128,4096]{1,0:T(8,128)(2,1)S(1)}, u32[]{:S(2)}, u32[]{:S(2)}) collective-permute-start(bf16[128,4096]{1,0:T(8,128)(2,1)} %rest_0_.5), channel_id=1, source_target_pairs={{0,1},{1,0},{2,3},{3,2},{4,5},{5,4},{6,7},{7,6},{8,9},{9,8},{10,11... | collective-permute-start | bytes 3145736 | tf_op jit(solution)/shard_map/ppermute | solution.py:392
  8.2 24.1 %copy-start = (bf16[128,4096]{1,0:T(8,128)(2,1)S(1)}, bf16[128,4096]{1,0:T(8,128)(2,1)}, u32[]{:S(2)}) copy-start(bf16[128,4096]{1,0:T(8,128)(2,1)} %rest_0_.5) | copy-start | bytes 3145732
  8.2 24.1 %copy-start.1 = (s32[6]{0:T(128)S(1)}, s32[6]{0:T(128)}, u32[]{:S(2)}) copy-start(s32[6]{0:T(128)} %tiles_ref.7) | copy-start | bytes 76
  8.2 24.1 %copy-start.2 = (s32[6]{0:T(128)S(1)}, s32[6]{0:T(128)}, u32[]{:S(2)}) copy-start(s32[6]{0:T(128)} %pad_ref.7) | copy-start | bytes 76
  8.2 24.1 %copy-start.5 = (s32[48]{0:T(128)S(1)}, s32[48]{0:T(128)}, u32[]{:S(2)}) copy-start(s32[48]{0:T(128)} %constant.43.clone.table_ref) | copy-start | bytes 580
  27.1 13.4 %collective-permute-start.5 = (bf16[64,4096]{1,0:T(8,128)(2,1)S(1)}, bf16[64,4096]{1,0:T(8,128)(2,1)S(1)}, u32[]{:S(2)}, u32[]{:S(2)}) collective-permute-start(bf16[64,4096]{1,0:T(8,128)(2,1)S(1)} %slice.24), channel_id=1, source_target_pairs={{0,2},{1,3},{4,6},{5,7},{6,4},{7,5},{8,10},{9,11},{10,8},{11,9},{1... | collective-permute-start | bytes 1572872 | tf_op jit(solution)/shard_map/ppermute | solution.py:385
  29.4 25.7 %copy-start.4 = (s32[48]{0:T(128)S(1)}, s32[48]{0:T(128)}, u32[]{:S(2)}) copy-start(s32[48]{0:T(128)} %constant.44.clone.table_ref) | copy-start | bytes 580
  29.4 18.7 %collective-permute-start.7 = (bf16[128,4096]{1,0:T(8,128)(2,1)S(1)}, bf16[128,4096]{1,0:T(8,128)(2,1)S(1)}, u32[]{:S(2)}, u32[]{:S(2)}) collective-permute-start(bf16[128,4096]{1,0:T(8,128)(2,1)S(1)} %broadcast_select_fusion), channel_id=1, source_target_pairs={{4,0},{5,9},{6,2},{7,11},{8,4},{9,13},{10,6},{11,15},{20,16},{21,2... | collective-permute-start | bytes 3145736 | tf_op jit(solution)/shard_map/ppermute | solution.py:385
  40.6 28.9 %copy-start.3 = (s32[48]{0:T(128)S(1)}, s32[48]{0:T(128)}, u32[]{:S(2)}) copy-start(s32[48]{0:T(128)} %constant.45.clone.table_ref) | copy-start | bytes 580
  40.6 12.5 %collective-permute-start.8 = (bf16[64,4096]{1,0:T(8,128)(2,1)S(1)}, bf16[64,4096]{1,0:T(8,128)(2,1)S(1)}, u32[]{:S(2)}, u32[]{:S(2)}) collective-permute-start(bf16[64,4096]{1,0:T(8,128)(2,1)S(1)} %slice.25), channel_id=1, source_target_pairs={{0,2},{1,3},{4,6},{5,7},{6,4},{7,5},{8,10},{9,11},{10,8},{11,9},{1... | collective-permute-start | bytes 1572872 | tf_op jit(solution)/shard_map/ppermute | solution.py:385
  42.7 23.7 %collective-permute-start.4 = (bf16[128,4096]{1,0:T(8,128)(2,1)}, bf16[128,4096]{1,0:T(8,128)(2,1)S(1)}, u32[]{:S(2)}, u32[]{:S(2)}) collective-permute-start(bf16[128,4096]{1,0:T(8,128)(2,1)} %collective-permute-done.3.rest_4_), channel_id=1, source_target_pairs={{2,6},{3,7},{4,0},{5,1},{6,10},{7,11},{8,4},{9,5},{10,14},{11,15},... | collective-permute-start | bytes 3145736 | tf_op jit(solution)/shard_map/ppermute | solution.py:385
  45.5 20.9 %collective-permute-start.6 = (bf16[64,4096]{1,0:T(8,128)(2,1)S(1)}, bf16[64,4096]{1,0:T(8,128)(2,1)S(1)}, u32[]{:S(2)}, u32[]{:S(2)}) collective-permute-start(bf16[64,4096]{1,0:T(8,128)(2,1)S(1)} %collective-permute-done.5.rest_2_), channel_id=1, source_target_pairs={{4,8},{5,9},{6,2},{7,3},{8,12},{9,13},{10,6},{11,7},{20,24},{21,25... | collective-permute-start | bytes 1572872 | tf_op jit(solution)/shard_map/ppermute | solution.py:385
  53.1 16.3 %collective-permute-start.9 = (bf16[64,4096]{1,0:T(8,128)(2,1)S(1)}, bf16[64,4096]{1,0:T(8,128)(2,1)S(1)}, u32[]{:S(2)}, u32[]{:S(2)}) collective-permute-start(bf16[64,4096]{1,0:T(8,128)(2,1)S(1)} %collective-permute-done.8.rest_3_), channel_id=1, source_target_pairs={{4,8},{5,9},{6,2},{7,3},{8,12},{9,13},{10,6},{11,7},{20,24},{21,25... | collective-permute-start | bytes 1572872 | tf_op jit(solution)/shard_map/ppermute | solution.py:385
  73.2 6.0 %collective-permute-start.10 = (bf16[128,4224]{1,0:T(8,128)(2,1)S(1)}, bf16[128,4224]{1,0:T(8,128)(2,1)S(1)}, u32[]{:S(2)}, u32[]{:S(2)}) collective-permute-start(bf16[128,4224]{1,0:T(8,128)(2,1)S(1)} %get-tuple-element.37), channel_id=1, source_target_pairs={{0,1},{1,0},{2,3},{3,2},{4,5},{5,4},{6,7},{7,6},{8,9},{9,8},{10,11... | collective-permute-start | bytes 3244040 | tf_op jit(solution)/shard_map/ppermute | solution.py:414

commit v5 on v4

--- a/solution.py
+++ b/solution.py
@@ -214,7 +214,7 @@
         weights[:, pl.ds(pl.multiple_of(b * wide, wide), wide)] = block
         den[...] += jnp.broadcast_to(jnp.sum(block.astype(jnp.float32), axis=1, keepdims=True), den.shape)
 
-    chunk = 512
+    chunk = 1024
 
     def products(depth):
         @pl.loop(0, width // chunk)
@@ -330,7 +330,7 @@
         def _(copy=copy):
             copy.wait()
 
-    chunk = 512
+    chunk = 1024
 
     @pl.loop(0, width // chunk)
     def _(f):

time: 81.7 us -> 81 us (level)
  Pallas kernels: 17.7 us -> 15.1 us
  waiting for transfers between devices: 34.9 us -> 36.4 us
    pallas_call x3, Pallas kernels: 15.3 us -> 13.4 us  [attend(): pl.pallas_call(functools.partial(attend_kernel, rows, bounds, cluster_til...]
    ppermute x9, waiting for transfers between devices: 34.9 us -> 35.8 us  [send(): held[name] = lax.ppermute(operand, 'tiles', pairs[name])]
  transfers between devices with their start and end apart: 11 -> 11, of which waited for: 6 -> 7; matrix products, arithmetic and copies ran while one was open for 0% -> 0% of each run, Pallas kernels for 17% -> 15%
where the time goes in v5:
time: 81 us; the launch traced here: 79.5 us
  waiting for transfers between devices  36.4 us (45%)
  starting transfers between devices  25.9 us (32%)
  Pallas kernels  15.1 us (19%)
  other arithmetic  1.8 us (2%)
    ppermute x9, waiting for transfers between devices, send(): held[name] = lax.ppermute(operand, 'tiles', pairs[name])  35.8 us
    ppermute x9, starting transfers between devices, send(): held[name] = lax.ppermute(operand, 'tiles', pairs[name])  20.9 us
    pallas_call x3, Pallas kernels, attend(): pl.pallas_call(functools.partial(attend_kernel, rows, bounds, cluster_til...  13.4 us
    ppermute x1, starting transfers between devices, body(): other_sum = lax.ppermute(sib_sum, 'tiles', cores)  3.37 us
    pallas_call x1, Pallas kernels, own_products(): pl.pallas_call(functools.partial(own_kernel, rows, depth // HALF, cluster...  1.76 us
  transfers between devices with their start and end apart: 11, of which 7 were waited for; matrix products, arithmetic and copies ran while one was open for 0% of the time, Pallas kernels for 15%

profile of v5, /device:TPU:17, one launch (start us, length us, event | category | flops | bytes accessed | tf_op | source)
XLA Modules:
  0.0 79.5 jit_solution(10852361943854881369)
XLA Ops:
  0.0 1.2 %collective-permute-start.3 = (bf16[128,4096]{1,0:T(8,128)(2,1)}, bf16[128,4096]{1,0:T(8,128)(2,1)}, u32[]{:S(2)}, u32[]{:S(2)}) collective-permute-start(bf16[128,4096]{1,0:T(8,128)(2,1)} %rest_0_.5), channel_id=1, source_target_pairs={{0,2},{1,3},{2,0},{3,1},{4,6},{5,7},{6,4},{7,5},{8,10},{9,11},{10,... | collective-permute-start | bytes 3145736 | tf_op jit(solution)/shard_map/ppermute | solution.py:385
  1.2 2.1 %collective-permute-start.2 = (bf16[128,4096]{1,0:T(8,128)(2,1)}, bf16[128,4096]{1,0:T(8,128)(2,1)S(1)}, u32[]{:S(2)}, u32[]{:S(2)}) collective-permute-start(bf16[128,4096]{1,0:T(8,128)(2,1)} %rest_0_.5), channel_id=1, source_target_pairs={{2,6},{3,7},{4,0},{5,1},{6,10},{7,11},{8,4},{9,5},{10,14},{11,15},... | collective-permute-start | bytes 3145736 | tf_op jit(solution)/shard_map/ppermute | solution.py:385
  3.3 3.3 %collective-permute-start.1 = (bf16[128,4096]{1,0:T(8,128)(2,1)}, bf16[128,4096]{1,0:T(8,128)(2,1)S(1)}, u32[]{:S(2)}, u32[]{:S(2)}) collective-permute-start(bf16[128,4096]{1,0:T(8,128)(2,1)} %rest_0_.5), channel_id=1, source_target_pairs={{0,4},{1,5},{4,8},{5,9},{6,2},{7,3},{8,12},{9,13},{10,6},{11,7},{1... | collective-permute-start | bytes 3145736 | tf_op jit(solution)/shard_map/ppermute | solution.py:385
  6.6 1.6 %collective-permute-start = (bf16[128,4096]{1,0:T(8,128)(2,1)}, bf16[128,4096]{1,0:T(8,128)(2,1)S(1)}, u32[]{:S(2)}, u32[]{:S(2)}) collective-permute-start(bf16[128,4096]{1,0:T(8,128)(2,1)} %rest_0_.5), channel_id=1, source_target_pairs={{0,1},{1,0},{2,3},{3,2},{4,5},{5,4},{6,7},{7,6},{8,9},{9,8},{10,11... | collective-permute-start | bytes 3145736 | tf_op jit(solution)/shard_map/ppermute | solution.py:392
  8.2 16.2 %collective-permute-done.3.rest_4_ = bf16[128,4096]{1,0:T(8,128)(2,1)} collective-permute-done((bf16[128,4096]{1,0:T(8,128)(2,1)}, bf16[128,4096]{1,0:T(8,128)(2,1)}, u32[]{:S(2)}, u32[]{:S(2)}) %collective-permute-start.3) | collective-permute-done | bytes 1048608 | tf_op jit(solution)/shard_map/ppermute | solution.py:385
  24.3 2.7 %collective-permute-done.2.rest_2_ = bf16[128,4096]{1,0:T(8,128)(2,1)S(1)} collective-permute-done((bf16[128,4096]{1,0:T(8,128)(2,1)}, bf16[128,4096]{1,0:T(8,128)(2,1)S(1)}, u32[]{:S(2)}, u32[]{:S(2)}) %collective-permute-start.2) | collective-permute-done | bytes 1048608 | tf_op jit(solution)/shard_map/ppermute | solution.py:385
  27.1 2.1 %collective-permute-start.5 = (bf16[64,4096]{1,0:T(8,128)(2,1)S(1)}, bf16[64,4096]{1,0:T(8,128)(2,1)S(1)}, u32[]{:S(2)}, u32[]{:S(2)}) collective-permute-start(bf16[64,4096]{1,0:T(8,128)(2,1)S(1)} %slice.24), channel_id=1, source_target_pairs={{0,2},{1,3},{4,6},{5,7},{6,4},{7,5},{8,10},{9,11},{10,8},{11,9},{1... | collective-permute-start | bytes 1572872 | tf_op jit(solution)/shard_map/ppermute | solution.py:385
  29.2 0.0 collective-permute-done.1.rest_3_
  29.2 0.0 collective-permute-done.rest_1_
  29.2 0.1 broadcast_select_fusion
  29.4 0.0 copy-start.4
  29.4 2.9 %collective-permute-start.7 = (bf16[128,4096]{1,0:T(8,128)(2,1)S(1)}, bf16[128,4096]{1,0:T(8,128)(2,1)S(1)}, u32[]{:S(2)}, u32[]{:S(2)}) collective-permute-start(bf16[128,4096]{1,0:T(8,128)(2,1)S(1)} %broadcast_select_fusion), channel_id=1, source_target_pairs={{4,0},{5,9},{6,2},{7,11},{8,4},{9,13},{10,6},{11,15},{20,16},{21,2... | collective-permute-start | bytes 3145736 | tf_op jit(solution)/shard_map/ppermute | solution.py:385
  32.3 6.8 %shard_map.73 = (f32[128,4352]{1,0:T(8,128)S(1)}, f32[128,4352]{1,0:T(8,128)S(1)}) custom-call(s32[6]{0:T(128)S(1)} %copy-done.1, s32[6]{0:T(128)S(1)} %copy-done.2, s32[48]{0:T(128)S(1)} %copy-done.5, bf16[128,4096]{1,0:T(8,128)(2,1)S(1)} %copy-done, bf16[128,4096]{1,0:T(8,128)(2,1)S(1)} %collective-permute-done.rest_1_, ...), custom_call_target="tpu_custom_call" | custom-call | flops 2147483648 | bytes 6291456 | tf_op jit(solution)/shard_map/pallas_call | solution.py:279
  39.1 1.4 %collective-permute-done.5.rest_2_ = bf16[64,4096]{1,0:T(8,128)(2,1)S(1)} collective-permute-done((bf16[64,4096]{1,0:T(8,128)(2,1)S(1)}, bf16[64,4096]{1,0:T(8,128)(2,1)S(1)}, u32[]{:S(2)}, u32[]{:S(2)}) %collective-permute-start.5) | collective-permute-done | bytes 524320 | tf_op jit(solution)/shard_map/ppermute | solution.py:385
  40.6 0.0 copy-start.3
  40.6 2.1 %collective-permute-start.8 = (bf16[64,4096]{1,0:T(8,128)(2,1)S(1)}, bf16[64,4096]{1,0:T(8,128)(2,1)S(1)}, u32[]{:S(2)}, u32[]{:S(2)}) collective-permute-start(bf16[64,4096]{1,0:T(8,128)(2,1)S(1)} %slice.25), channel_id=1, source_target_pairs={{0,2},{1,3},{4,6},{5,7},{6,4},{7,5},{8,10},{9,11},{10,8},{11,9},{1... | collective-permute-start | bytes 1572872 | tf_op jit(solution)/shard_map/ppermute | solution.py:385
  42.7 2.1 %collective-permute-start.4 = (bf16[128,4096]{1,0:T(8,128)(2,1)}, bf16[128,4096]{1,0:T(8,128)(2,1)S(1)}, u32[]{:S(2)}, u32[]{:S(2)}) collective-permute-start(bf16[128,4096]{1,0:T(8,128)(2,1)} %collective-permute-done.3.rest_4_), channel_id=1, source_target_pairs={{2,6},{3,7},{4,0},{5,1},{6,10},{7,11},{8,4},{9,5},{10,14},{11,15},... | collective-permute-start | bytes 3145736 | tf_op jit(solution)/shard_map/ppermute | solution.py:385
  44.8 3.3 %collective-permute-start.6 = (bf16[64,4096]{1,0:T(8,128)(2,1)S(1)}, bf16[64,4096]{1,0:T(8,128)(2,1)S(1)}, u32[]{:S(2)}, u32[]{:S(2)}) collective-permute-start(bf16[64,4096]{1,0:T(8,128)(2,1)S(1)} %collective-permute-done.5.rest_2_), channel_id=1, source_target_pairs={{4,8},{5,9},{6,2},{7,3},{8,12},{9,13},{10,6},{11,7},{20,24},{21,25... | collective-permute-start | bytes 1572872 | tf_op jit(solution)/shard_map/ppermute | solution.py:385
  48.1 0.0 collective-permute-done.7.rest_4_
  48.1 5.0 %collective-permute-done.8.rest_3_ = bf16[64,4096]{1,0:T(8,128)(2,1)S(1)} collective-permute-done((bf16[64,4096]{1,0:T(8,128)(2,1)S(1)}, bf16[64,4096]{1,0:T(8,128)(2,1)S(1)}, u32[]{:S(2)}, u32[]{:S(2)}) %collective-permute-start.8) | collective-permute-done | bytes 524320 | tf_op jit(solution)/shard_map/ppermute | solution.py:385
  53.1 1.9 %collective-permute-start.9 = (bf16[64,4096]{1,0:T(8,128)(2,1)S(1)}, bf16[64,4096]{1,0:T(8,128)(2,1)S(1)}, u32[]{:S(2)}, u32[]{:S(2)}) collective-permute-start(bf16[64,4096]{1,0:T(8,128)(2,1)S(1)} %collective-permute-done.8.rest_3_), channel_id=1, source_target_pairs={{4,8},{5,9},{6,2},{7,3},{8,12},{9,13},{10,6},{11,7},{20,24},{21,25... | collective-permute-start | bytes 1572872 | tf_op jit(solution)/shard_map/ppermute | solution.py:385
  55.0 3.4 %shard_map.74 = (f32[128,4352]{1,0:T(8,128)S(1)}, f32[128,4352]{1,0:T(8,128)S(1)}) custom-call(s32[6]{0:T(128)S(1)} %copy-done.1, s32[6]{0:T(128)S(1)} %copy-done.2, s32[48]{0:T(128)S(1)} %copy-done.4, bf16[128,4096]{1,0:T(8,128)(2,1)S(1)} %copy-done, bf16[128,4096]{1,0:T(8,128)(2,1)S(1)} %collective-permute-done.rest_1_, ...), custom_call_target="tpu_custom_call" | custom-call | flops 1073741824 | bytes 4194304 | tf_op jit(solution)/shard_map/pallas_call | solution.py:279
  58.5 8.0 %collective-permute-done.4.rest_2_.rest_0_ = bf16[128,4096]{1,0:T(8,128)(2,1)S(1)} collective-permute-done((bf16[128,4096]{1,0:T(8,128)(2,1)}, bf16[128,4096]{1,0:T(8,128)(2,1)S(1)}, u32[]{:S(2)}, u32[]{:S(2)}) %collective-permute-start.4) | collective-permute-done | bytes 1048608 | tf_op jit(solution)/shard_map/ppermute | solution.py:385
  66.4 0.0 collective-permute-done.6.rest_3_.rest_1_
  66.4 2.6 %collective-permute-done.9.rest_4_.rest_2_ = bf16[64,4096]{1,0:T(8,128)(2,1)S(1)} collective-permute-done((bf16[64,4096]{1,0:T(8,128)(2,1)S(1)}, bf16[64,4096]{1,0:T(8,128)(2,1)S(1)}, u32[]{:S(2)}, u32[]{:S(2)}) %collective-permute-start.9) | collective-permute-done | bytes 524320 | tf_op jit(solution)/shard_map/ppermute | solution.py:385
  69.0 3.1 %shard_map.75 = (bf16[128,256]{1,0:T(8,128)(2,1)S(1)}, f32[128,128]{1,0:T(8,128)S(1)}, bf16[128,4224]{1,0:T(8,128)(2,1)S(1)}) custom-call(s32[6]{0:T(128)S(1)} %copy-done.1, s32[6]{0:T(128)S(1)} %copy-done.2, s32[48]{0:T(128)S(1)} %copy-done.3, bf16[128,4096]{1,0:T(8,128)(2,1)S(1)} %copy-done, bf16[128,4096]{1,0:T(8,128)(2,1)S(1)} %collective-permute-done.rest_1_, ...), custom_call_target="tpu_custom_call" | custom-call | flops 1073741824 | bytes 4194304 | tf_op jit(solution)/shard_map/pallas_call | solution.py:279
  72.1 3.4 %collective-permute-start.10 = (bf16[128,4224]{1,0:T(8,128)(2,1)S(1)}, bf16[128,4224]{1,0:T(8,128)(2,1)S(1)}, u32[]{:S(2)}, u32[]{:S(2)}) collective-permute-start(bf16[128,4224]{1,0:T(8,128)(2,1)S(1)} %get-tuple-element.37), channel_id=1, source_target_pairs={{0,1},{1,0},{2,3},{3,2},{4,5},{5,4},{6,7},{7,6},{8,9},{9,8},{10,11... | collective-permute-start | bytes 3244040 | tf_op jit(solution)/shard_map/ppermute | solution.py:414
  75.5 1.8 %shard_map.76 = f32[128,4096]{1,0:T(8,128)S(1)} custom-call(s32[6]{0:T(128)S(1)} %copy-done.1, s32[6]{0:T(128)S(1)} %copy-done.2, s32[48]{0:T(128)S(1)} %copy-done.3, bf16[128,4096]{1,0:T(8,128)(2,1)S(1)} %collective-permute-done.4.rest_2_.rest_0_, bf16[64,4096]{1,0:T(8,128)(2,1)S(1)} %collective-permute-done.6.rest_3_.rest_1_, ...), custom_call_target="tpu_custom_call" | custom-call | flops 268435456 | bytes 2097152 | tf_op jit(solution)/shard_map/pallas_call | solution.py:349
  77.3 0.6 collective-permute-done.10
  77.8 0.2 compare_reduce_fusion
  78.0 0.1 fusion
  78.1 1.4 %select_convert_fusion = bf16[128,4096]{1,0:T(8,128)(2,1)} fusion(f32[128,4096]{1,0:T(8,128)S(1)} %shard_map.76, bf16[128,4224]{1,0:T(8,128)(2,1)S(1)} %collective-permute-done.10, f32[128]{0:T(128)S(1)} %fusion, pred[128]{0:T(512)(128)(4,1)S(1)} %get-tuple-element.39), kind=kLoop, calls=%fused_computation | loop fusion | flops 2621440 | bytes 4194944 | tf_op jit(solution)/shard_map/convert_element_type | solution.py:420
  (13 shorter events, 0.1 us)
Async XLA Ops:
  0.0 24.3 %collective-permute-start.3 = (bf16[128,4096]{1,0:T(8,128)(2,1)}, bf16[128,4096]{1,0:T(8,128)(2,1)}, u32[]{:S(2)}, u32[]{:S(2)}) collective-permute-start(bf16[128,4096]{1,0:T(8,128)(2,1)} %rest_0_.5), channel_id=1, source_target_pairs={{0,2},{1,3},{2,0},{3,1},{4,6},{5,7},{6,4},{7,5},{8,10},{9,11},{10,... | collective-permute-start | bytes 3145736 | tf_op jit(solution)/shard_map/ppermute | solution.py:385
  1.2 25.8 %collective-permute-start.2 = (bf16[128,4096]{1,0:T(8,128)(2,1)}, bf16[128,4096]{1,0:T(8,128)(2,1)S(1)}, u32[]{:S(2)}, u32[]{:S(2)}) collective-permute-start(bf16[128,4096]{1,0:T(8,128)(2,1)} %rest_0_.5), channel_id=1, source_target_pairs={{2,6},{3,7},{4,0},{5,1},{6,10},{7,11},{8,4},{9,5},{10,14},{11,15},... | collective-permute-start | bytes 3145736 | tf_op jit(solution)/shard_map/ppermute | solution.py:385
  3.3 25.9 %collective-permute-start.1 = (bf16[128,4096]{1,0:T(8,128)(2,1)}, bf16[128,4096]{1,0:T(8,128)(2,1)S(1)}, u32[]{:S(2)}, u32[]{:S(2)}) collective-permute-start(bf16[128,4096]{1,0:T(8,128)(2,1)} %rest_0_.5), channel_id=1, source_target_pairs={{0,4},{1,5},{4,8},{5,9},{6,2},{7,3},{8,12},{9,13},{10,6},{11,7},{1... | collective-permute-start | bytes 3145736 | tf_op jit(solution)/shard_map/ppermute | solution.py:385
  6.6 22.6 %collective-permute-start = (bf16[128,4096]{1,0:T(8,128)(2,1)}, bf16[128,4096]{1,0:T(8,128)(2,1)S(1)}, u32[]{:S(2)}, u32[]{:S(2)}) collective-permute-start(bf16[128,4096]{1,0:T(8,128)(2,1)} %rest_0_.5), channel_id=1, source_target_pairs={{0,1},{1,0},{2,3},{3,2},{4,5},{5,4},{6,7},{7,6},{8,9},{9,8},{10,11... | collective-permute-start | bytes 3145736 | tf_op jit(solution)/shard_map/ppermute | solution.py:392
  8.2 24.1 %copy-start = (bf16[128,4096]{1,0:T(8,128)(2,1)S(1)}, bf16[128,4096]{1,0:T(8,128)(2,1)}, u32[]{:S(2)}) copy-start(bf16[128,4096]{1,0:T(8,128)(2,1)} %rest_0_.5) | copy-start | bytes 3145732
  8.2 24.1 %copy-start.1 = (s32[6]{0:T(128)S(1)}, s32[6]{0:T(128)}, u32[]{:S(2)}) copy-start(s32[6]{0:T(128)} %tiles_ref.7) | copy-start | bytes 76
  8.2 24.1 %copy-start.2 = (s32[6]{0:T(128)S(1)}, s32[6]{0:T(128)}, u32[]{:S(2)}) copy-start(s32[6]{0:T(128)} %pad_ref.7) | copy-start | bytes 76
  8.2 24.1 %copy-start.5 = (s32[48]{0:T(128)S(1)}, s32[48]{0:T(128)}, u32[]{:S(2)}) copy-start(s32[48]{0:T(128)} %constant.43.clone.table_ref) | copy-start | bytes 580
  27.1 13.4 %collective-permute-start.5 = (bf16[64,4096]{1,0:T(8,128)(2,1)S(1)}, bf16[64,4096]{1,0:T(8,128)(2,1)S(1)}, u32[]{:S(2)}, u32[]{:S(2)}) collective-permute-start(bf16[64,4096]{1,0:T(8,128)(2,1)S(1)} %slice.24), channel_id=1, source_target_pairs={{0,2},{1,3},{4,6},{5,7},{6,4},{7,5},{8,10},{9,11},{10,8},{11,9},{1... | collective-permute-start | bytes 1572872 | tf_op jit(solution)/shard_map/ppermute | solution.py:385
  29.4 25.7 %copy-start.4 = (s32[48]{0:T(128)S(1)}, s32[48]{0:T(128)}, u32[]{:S(2)}) copy-start(s32[48]{0:T(128)} %constant.44.clone.table_ref) | copy-start | bytes 580
  29.4 18.7 %collective-permute-start.7 = (bf16[128,4096]{1,0:T(8,128)(2,1)S(1)}, bf16[128,4096]{1,0:T(8,128)(2,1)S(1)}, u32[]{:S(2)}, u32[]{:S(2)}) collective-permute-start(bf16[128,4096]{1,0:T(8,128)(2,1)S(1)} %broadcast_select_fusion), channel_id=1, source_target_pairs={{4,0},{5,9},{6,2},{7,11},{8,4},{9,13},{10,6},{11,15},{20,16},{21,2... | collective-permute-start | bytes 3145736 | tf_op jit(solution)/shard_map/ppermute | solution.py:385
  40.6 28.4 %copy-start.3 = (s32[48]{0:T(128)S(1)}, s32[48]{0:T(128)}, u32[]{:S(2)}) copy-start(s32[48]{0:T(128)} %constant.45.clone.table_ref) | copy-start | bytes 580
  40.6 12.5 %collective-permute-start.8 = (bf16[64,4096]{1,0:T(8,128)(2,1)S(1)}, bf16[64,4096]{1,0:T(8,128)(2,1)S(1)}, u32[]{:S(2)}, u32[]{:S(2)}) collective-permute-start(bf16[64,4096]{1,0:T(8,128)(2,1)S(1)} %slice.25), channel_id=1, source_target_pairs={{0,2},{1,3},{4,6},{5,7},{6,4},{7,5},{8,10},{9,11},{10,8},{11,9},{1... | collective-permute-start | bytes 1572872 | tf_op jit(solution)/shard_map/ppermute | solution.py:385
  42.7 23.7 %collective-permute-start.4 = (bf16[128,4096]{1,0:T(8,128)(2,1)}, bf16[128,4096]{1,0:T(8,128)(2,1)S(1)}, u32[]{:S(2)}, u32[]{:S(2)}) collective-permute-start(bf16[128,4096]{1,0:T(8,128)(2,1)} %collective-permute-done.3.rest_4_), channel_id=1, source_target_pairs={{2,6},{3,7},{4,0},{5,1},{6,10},{7,11},{8,4},{9,5},{10,14},{11,15},... | collective-permute-start | bytes 3145736 | tf_op jit(solution)/shard_map/ppermute | solution.py:385
  44.8 21.6 %collective-permute-start.6 = (bf16[64,4096]{1,0:T(8,128)(2,1)S(1)}, bf16[64,4096]{1,0:T(8,128)(2,1)S(1)}, u32[]{:S(2)}, u32[]{:S(2)}) collective-permute-start(bf16[64,4096]{1,0:T(8,128)(2,1)S(1)} %collective-permute-done.5.rest_2_), channel_id=1, source_target_pairs={{4,8},{5,9},{6,2},{7,3},{8,12},{9,13},{10,6},{11,7},{20,24},{21,25... | collective-permute-start | bytes 1572872 | tf_op jit(solution)/shard_map/ppermute | solution.py:385
  53.1 15.9 %collective-permute-start.9 = (bf16[64,4096]{1,0:T(8,128)(2,1)S(1)}, bf16[64,4096]{1,0:T(8,128)(2,1)S(1)}, u32[]{:S(2)}, u32[]{:S(2)}) collective-permute-start(bf16[64,4096]{1,0:T(8,128)(2,1)S(1)} %collective-permute-done.8.rest_3_), channel_id=1, source_target_pairs={{4,8},{5,9},{6,2},{7,3},{8,12},{9,13},{10,6},{11,7},{20,24},{21,25... | collective-permute-start | bytes 1572872 | tf_op jit(solution)/shard_map/ppermute | solution.py:385
  72.1 5.7 %collective-permute-start.10 = (bf16[128,4224]{1,0:T(8,128)(2,1)S(1)}, bf16[128,4224]{1,0:T(8,128)(2,1)S(1)}, u32[]{:S(2)}, u32[]{:S(2)}) collective-permute-start(bf16[128,4224]{1,0:T(8,128)(2,1)S(1)} %get-tuple-element.37), channel_id=1, source_target_pairs={{0,1},{1,0},{2,3},{3,2},{4,5},{5,4},{6,7},{7,6},{8,9},{9,8},{10,11... | collective-permute-start | bytes 3244040 | tf_op jit(solution)/shard_map/ppermute | solution.py:414
